TPU v7x, 32 devices: a whole 2x2x4 slice. The times are simulated.
32 devices in a mesh: dp: 4 (over z), row: 4 (over y, x), col: 2 (over core).
Axes of the slice: x: 2, y: 2, z: 4, core: 2. Of those that a mesh axis runs over, the one named last changes fastest.
Arguments:
- hidden_in: bfloat16 [16384, 1024], P(('dp', 'row')), may hold values from -6 to 6
- segments: int32 [16384], P(('dp', 'row')), may hold values from 0 to 6, as said below
- mixer_gain: bfloat16 [1024], P(('dp', 'row')), may hold values from 0.25 to 1.75
- ssm_inner: bfloat16 [1024, 2, 1536], P(('dp', 'row'), None, 'col'), may hold values from -0.1875 to 0.1875
- state_proj: bfloat16 [1024, 256], P(('dp', 'row')), may hold values from -0.1875 to 0.1875
- step_proj: bfloat16 [1024, 24], P(('dp', 'row'), 'col'), may hold values from -0.1875 to 0.1875
- query_proj: bfloat16 [1024, 512], P(('dp', 'row'), 'col'), may hold values from -0.1875 to 0.1875
- key_value_projection: bfloat16 [1024, 2, 128], P(('dp', 'row'), None, 'col'), may hold values from -0.1875 to 0.1875
- conv_inner: float32 [4, 1536], P(None, 'col'), may hold values from -2.5 to 2.5
- conv_state: float32 [4, 256], replicated, may hold values from -2.5 to 2.5
- step_bias: float32 [24], P('col'), may hold values from -6 to -2
- decay_log: float32 [24], P('col'), may hold values from 0 to 3
- skip_gain: float32 [24], P('col'), may hold values from 0.5 to 1.5
- ssm_out: bfloat16 [1536, 1024], P('col', ('dp', 'row')), may hold values from -0.15625 to 0.15625
- attn_out: bfloat16 [512, 1024], P('col', ('dp', 'row')), may hold values from -1 to 1
- ffn_gain: bfloat16 [1024], P(('dp', 'row')), may hold values from 0.25 to 1.75
- gate_up: bfloat16 [1024, 2, 2048], P(('dp', 'row'), None, 'col'), may hold values from -0.1875 to 0.1875
- down_proj: bfloat16 [2048, 1024], P('col', ('dp', 'row')), may hold values from -0.125 to 0.125
- output_cotangent: bfloat16 [16384, 1024], P(('dp', 'row')), may hold values from -6 to 6
Outputs:
- hidden_out: bfloat16 [16384, 1024], P(('dp', 'row'))
- input_grad: float32 [16384, 1024], P(('dp', 'row'))
- grad_mixer_gain: float32 [1024], P(('dp', 'row'))
- grad_ssm_inner: float32 [1024, 2, 1536], P(('dp', 'row'), None, 'col')
- grad_state_proj: float32 [1024, 256], P(('dp', 'row'))
- grad_step_proj: float32 [1024, 24], P(('dp', 'row'), 'col')
- grad_query_proj: float32 [1024, 512], P(('dp', 'row'), 'col')
- grad_keyval_proj: float32 [1024, 2, 128], P(('dp', 'row'), None, 'col')
- grad_conv_inner: float32 [4, 1536], P(None, 'col')
- conv_state_gradient: float32 [4, 256], replicated
- grad_step_bias: float32 [24], P('col')
- grad_decay_log: float32 [24], P('col')
- grad_skip_gain: float32 [24], P('col')
- grad_ssm_out: float32 [1536, 1024], P('col', ('dp', 'row'))
- grad_attn_out: float32 [512, 1024], P('col', ('dp', 'row'))
- grad_ffn_gain: float32 [1024], P(('dp', 'row'))
- grad_gate_up: float32 [1024, 2, 2048], P(('dp', 'row'), None, 'col')
- grad_down_proj: float32 [2048, 1024], P('col', ('dp', 'row'))
Inputs may be any that keep to these rules, and one draw needn't show every extreme that they name: `segments`: within each 1024-token sequence (tokens k * 1024 onward) the numbers start at 0, never fall and rise by one where a document starts; a document that starts and ends inside the sequence has 204 tokens or more.
All inputs are finite; a program needn't handle non-finite values.
Results may differ from a plain program's by a relative error of at most 0.018.
Values may be sent and summed in bfloat16 or wider, within the bound.
A program may use at most 320 MiB of HBM per device.

v0:
```python
import jax
import jax.numpy as jnp
from jax import lax
from jax.sharding import PartitionSpec as P

HEAD_SIZE = 64
SEQ_LEN = 1024
SPAN = 256
QBLOCK = 512


EPS = 1e-05
THETA = 100000000000.0
HIGH = lax.Precision.HIGHEST


def causal_conv(signal, kernel, segment_ids):
    length = signal.shape[0]
    kernel_width = kernel.shape[0]
    summed = signal * kernel[kernel_width - 1][None, :]
    for offset in range(1, kernel_width):
        shifted = jnp.concatenate(
            [jnp.zeros((offset, signal.shape[1]), signal.dtype), signal[: length - offset]], 0
        )
        earlier = jnp.concatenate(
            [jnp.full((offset,), -1, segment_ids.dtype), segment_ids[: length - offset]], 0
        )
        matches = (earlier == segment_ids).astype(signal.dtype)
        summed = summed + shifted * kernel[kernel_width - 1 - offset][None, :] * matches[:, None]
    return summed


def state_scan(inner_heads, input_map, output_map, step_size, decay_rate, segment_ids):
    length, head_count, head_width = inner_heads.shape
    blocks = length // SPAN
    log_decay = step_size * decay_rate[None, :]
    inner_blocks = inner_heads.reshape(blocks, SPAN, head_count, head_width)
    input_blocks = input_map.reshape(blocks, SPAN, -1)
    output_blocks = output_map.reshape(blocks, SPAN, -1)
    step_blocks = step_size.reshape(blocks, SPAN, head_count)
    decay_blocks = log_decay.reshape(blocks, SPAN, head_count)
    segment_blocks = segment_ids.reshape(blocks, SPAN)
    previous = jnp.concatenate([segment_ids[:1], segment_blocks[:-1, -1]], 0)
    causal = jnp.arange(SPAN)[:, None] >= jnp.arange(SPAN)[None, :]

    def advance(carried, pieces):
        inner_part, input_part, output_part, step_part, decay_part, segment_part, before = pieces
        running = jnp.cumsum(decay_part, axis=0)
        spread = jnp.minimum(running[:, None, :] - running[None, :, :], 0.0)
        linked = (segment_part[:, None] == segment_part[None, :]) & causal
        kernel = jnp.where(linked[:, :, None], jnp.exp(spread), 0.0)
        intersection = jnp.dot(output_part, input_part.T, precision=HIGH)
        weights = kernel * intersection[:, :, None] * step_part[None, :, :]
        local_part = jnp.einsum("tsh,shp->thp", weights, inner_part, precision=HIGH)
        entering = (segment_part == before).astype(running.dtype)[:, None] * jnp.exp(running)
        from_state = (
            jnp.einsum("tn,hpn->thp", output_part, carried, precision=HIGH) * entering[:, :, None]
        )
        keeping = (segment_part[-1] == before).astype(running.dtype) * jnp.exp(running[-1])
        leaving = (
            (segment_part == segment_part[-1]).astype(running.dtype)[:, None]
            * jnp.exp(running[-1][None, :] - running)
            * step_part
        )
        updated = carried * keeping[:, None, None] + jnp.einsum(
            "sh,shp,sn->hpn", leaving, inner_part, input_part, precision=HIGH
        )
        return (updated, local_part + from_state)

    initial = jnp.zeros((head_count, head_width, input_map.shape[1]), inner_heads.dtype)
    _, outputs = lax.scan(
        advance,
        initial,
        (
            inner_blocks,
            input_blocks,
            output_blocks,
            step_blocks,
            decay_blocks,
            segment_blocks,
            previous,
        ),
    )
    return outputs.reshape(length, head_count, head_width)


def rotate(values):
    half_width = values.shape[-1] // 2
    position = jnp.arange(values.shape[0], dtype=jnp.float32)
    frequency = THETA ** (-2.0 * jnp.arange(half_width, dtype=jnp.float32) / values.shape[-1])
    angles = position[:, None] * frequency[None, :]
    cosine = jnp.cos(angles)[:, None, :]
    sine_part = jnp.sin(angles)[:, None, :]
    first_half = values[..., :half_width]
    second = values[..., half_width:]
    return jnp.concatenate(
        [first_half * cosine - second * sine_part, second * cosine + first_half * sine_part], -1
    )


def attention(queries, keys_in, values_in, segment_ids):
    length, query_heads, head_width = queries.shape
    key_heads = keys_in.shape[1]
    grouped = queries.reshape(length, key_heads, query_heads // key_heads, head_width)
    position = jnp.arange(length, dtype=jnp.int32)
    score_scale = head_width ** (-0.5)

    def row_block(start):
        query_rows = lax.dynamic_slice_in_dim(grouped, start, QBLOCK, 0)
        segment_rows = lax.dynamic_slice_in_dim(segment_ids, start, QBLOCK, 0)
        row_positions = start + jnp.arange(QBLOCK, dtype=jnp.int32)
        scores = jnp.einsum("tkge,ske->kgts", query_rows, keys_in, precision=HIGH) * score_scale
        allowed = (segment_rows[:, None] == segment_ids[None, :]) & (
            row_positions[:, None] >= position[None, :]
        )
        scores = jnp.where(allowed, scores, -1e30)
        highest = jnp.max(scores, axis=-1, keepdims=True)
        weights = jnp.exp(scores - highest)
        weights = weights / jnp.sum(weights, axis=-1, keepdims=True)
        return jnp.einsum("kgts,ske->tkge", weights, values_in, precision=HIGH)

    starts = jnp.arange(length // QBLOCK, dtype=jnp.int32) * QBLOCK
    blocks = lax.map(jax.checkpoint(row_block), starts)
    return blocks.reshape(length, query_heads * head_width)


def mixer(
    inner_gate,
    state_in,
    step_raw,
    query,
    keyval,
    conv_inner,
    conv_state,
    step_bias,
    decay_log,
    skip_gain,
    segment_ids,
):
    length = inner_gate.shape[0]
    inner_width = inner_gate.shape[1] // 2
    head_count = step_raw.shape[1]
    gate_in = inner_gate[:, :inner_width]
    inner = jax.nn.silu(causal_conv(inner_gate[:, inner_width:], conv_inner, segment_ids))
    maps = jax.nn.silu(causal_conv(state_in, conv_state, segment_ids))
    state_width = maps.shape[1] // 2
    step_size = jax.nn.softplus(step_raw + step_bias[None, :])
    decay_rate = -jnp.exp(decay_log)
    inner_heads = inner.reshape(length, head_count, HEAD_SIZE)
    scanned = state_scan(
        inner_heads,
        maps[:, :state_width],
        maps[:, state_width:],
        step_size,
        decay_rate,
        segment_ids,
    )
    scanned = scanned + skip_gain[None, :, None] * inner_heads
    ssm_part = scanned.reshape(length, inner_width) * jax.nn.silu(gate_in)
    kv_width = keyval.shape[1] // 2
    queries = rotate(query.reshape(length, -1, HEAD_SIZE))
    keys_in = rotate(keyval[:, :kv_width].reshape(length, -1, HEAD_SIZE))
    values_in = keyval[:, kv_width:].reshape(length, -1, HEAD_SIZE)
    attended = attention(queries, keys_in, values_in, segment_ids)
    return jnp.concatenate([ssm_part, attended], 1)


def rms_norm(values, gain):
    return values * lax.rsqrt(jnp.mean(values * values, axis=-1, keepdims=True) + EPS) * gain


def norm_back(values, gain, grad_normed):
    _, pullback = jax.vjp(rms_norm, values, gain)
    return pullback(grad_normed)


def matmul(left, right):
    return jnp.dot(left, right, preferred_element_type=jnp.float32)


def transposed_left(left, right):
    return lax.dot_general(
        left, right, (((0,), (0,)), ((), ())), preferred_element_type=jnp.float32
    )


def transposed_right(left, right):
    return lax.dot_general(
        left, right, (((1,), (1,)), ((), ())), preferred_element_type=jnp.float32
    )


def branch_total(partial_value):
    return lax.psum(partial_value.astype(jnp.bfloat16), "col").astype(jnp.float32)


def normed_total(partial_value):
    return lax.psum(partial_value, "col")


def local(
    hidden_in,
    segments,
    mixer_gain,
    ssm_inner,
    state_proj,
    step_proj,
    query_proj,
    key_value_projection,
    conv_inner,
    conv_state,
    step_bias,
    decay_log,
    skip_gain,
    ssm_out,
    attn_out,
    ffn_gain,
    gate_up,
    down_proj,
    output_cotangent,
):
    gathered_in = (
        lax.all_gather(mixer_gain, ("dp", "row"), axis=0, tiled=True),
        lax.all_gather(ssm_inner, ("dp", "row"), axis=0, tiled=True),
        lax.all_gather(state_proj, ("dp", "row"), axis=0, tiled=True),
        lax.all_gather(step_proj, ("dp", "row"), axis=0, tiled=True),
        lax.all_gather(query_proj, ("dp", "row"), axis=0, tiled=True),
        lax.all_gather(key_value_projection, ("dp", "row"), axis=0, tiled=True),
        lax.all_gather(ffn_gain, ("dp", "row"), axis=0, tiled=True),
        lax.all_gather(gate_up, ("dp", "row"), axis=0, tiled=True),
    )
    gathered_out = (
        lax.all_gather(ssm_out, ("dp", "row"), axis=1, tiled=True),
        lax.all_gather(attn_out, ("dp", "row"), axis=1, tiled=True),
        lax.all_gather(down_proj, ("dp", "row"), axis=1, tiled=True),
    )
    (
        gain_mixer,
        inner_weight,
        state_weight,
        step_weight,
        query_weight,
        keyval_weight,
        gain_ffn,
        gate_weight,
    ) = gathered_in
    ssm_weight, attn_weight, down_weight = gathered_out
    row_count = hidden_in.shape[0]
    model_width = hidden_in.shape[1]
    seq_count = row_count // SEQ_LEN
    segment_rows = segments.reshape(seq_count, SEQ_LEN)
    hidden = hidden_in.astype(jnp.float32)
    normed = rms_norm(hidden, gain_mixer.astype(jnp.float32)).astype(jnp.bfloat16)
    inner_gate = matmul(normed, inner_weight.reshape(model_width, -1))
    state_in = matmul(normed, state_weight)
    step_raw = matmul(normed, step_weight)
    query_in = matmul(normed, query_weight)
    keyval_in = matmul(normed, keyval_weight.reshape(model_width, -1))

    def local_mixer(
        inner_part,
        state_part,
        step_part,
        query_part,
        keyval_part,
        inner_kernel,
        state_kernel,
        bias_part,
        decay_part,
        skip_part,
    ):

        def single(leading_input, second_in, third_in, fourth_in, fifth_in, sequence_ids):
            return mixer(
                leading_input,
                second_in,
                third_in,
                fourth_in,
                fifth_in,
                inner_kernel,
                state_kernel,
                bias_part,
                decay_part,
                skip_part,
                sequence_ids,
            )

        mixed_rows = jax.vmap(single)(
            inner_part.reshape(seq_count, SEQ_LEN, -1),
            state_part.reshape(seq_count, SEQ_LEN, -1),
            step_part.reshape(seq_count, SEQ_LEN, -1),
            query_part.reshape(seq_count, SEQ_LEN, -1),
            keyval_part.reshape(seq_count, SEQ_LEN, -1),
            segment_rows,
        )
        return mixed_rows.reshape(row_count, -1)

    mixed_float, mixer_pull = jax.vjp(
        local_mixer,
        inner_gate,
        state_in,
        step_raw,
        query_in,
        keyval_in,
        conv_inner,
        conv_state,
        step_bias,
        decay_log,
        skip_gain,
    )
    mixed_out = mixed_float.astype(jnp.bfloat16)
    ssm_width = ssm_weight.shape[0]
    mixer_delta = branch_total(
        matmul(mixed_out[:, :ssm_width], ssm_weight) + matmul(mixed_out[:, ssm_width:], attn_weight)
    )
    middle = hidden + mixer_delta
    normed_ffn = rms_norm(middle, gain_ffn.astype(jnp.float32)).astype(jnp.bfloat16)
    gate_values = matmul(normed_ffn, gate_weight.reshape(model_width, -1))
    half_width = gate_values.shape[1] // 2
    gate_part = gate_values[:, :half_width]
    up_part = gate_values[:, half_width:]
    hidden_ffn = (jax.nn.silu(gate_part) * up_part).astype(jnp.bfloat16)
    result = middle + branch_total(matmul(hidden_ffn, down_weight))
    hidden_out = result.astype(jnp.bfloat16)
    gathered_in = (
        lax.all_gather(mixer_gain, ("dp", "row"), axis=0, tiled=True),
        lax.all_gather(ssm_inner, ("dp", "row"), axis=0, tiled=True),
        lax.all_gather(state_proj, ("dp", "row"), axis=0, tiled=True),
        lax.all_gather(step_proj, ("dp", "row"), axis=0, tiled=True),
        lax.all_gather(query_proj, ("dp", "row"), axis=0, tiled=True),
        lax.all_gather(key_value_projection, ("dp", "row"), axis=0, tiled=True),
        lax.all_gather(ffn_gain, ("dp", "row"), axis=0, tiled=True),
        lax.all_gather(gate_up, ("dp", "row"), axis=0, tiled=True),
    )
    gathered_out = (
        lax.all_gather(ssm_out, ("dp", "row"), axis=1, tiled=True),
        lax.all_gather(attn_out, ("dp", "row"), axis=1, tiled=True),
        lax.all_gather(down_proj, ("dp", "row"), axis=1, tiled=True),
    )
    (
        gain_mixer,
        inner_weight,
        state_weight,
        step_weight,
        query_weight,
        keyval_weight,
        gain_ffn,
        gate_weight,
    ) = gathered_in
    ssm_weight, attn_weight, down_weight = gathered_out
    grad_down = transposed_left(hidden_ffn, output_cotangent)
    grad_hidden_ffn = (
        transposed_right(output_cotangent, down_weight).astype(jnp.bfloat16).astype(jnp.float32)
    )
    sigmoid_gate = jax.nn.sigmoid(gate_part)
    grad_gate = grad_hidden_ffn * up_part * sigmoid_gate * (1.0 + gate_part * (1.0 - sigmoid_gate))
    grad_up = grad_hidden_ffn * gate_part * sigmoid_gate
    grad_gate_values = jnp.concatenate([grad_gate, grad_up], 1).astype(jnp.bfloat16)
    grad_gate_weight = transposed_left(normed_ffn, grad_gate_values)
    grad_normed_ffn = normed_total(
        transposed_right(grad_gate_values, gate_weight.reshape(model_width, -1))
    )
    back_middle, grad_gain_ffn = norm_back(middle, gain_ffn.astype(jnp.float32), grad_normed_ffn)
    grad_middle = output_cotangent.astype(jnp.float32) + back_middle
    grad_delta = grad_middle.astype(jnp.bfloat16)
    grad_ssm_weight = transposed_left(mixed_out[:, :ssm_width], grad_delta)
    grad_attn_weight = transposed_left(mixed_out[:, ssm_width:], grad_delta)
    grad_mixed = jnp.concatenate(
        [transposed_right(grad_delta, ssm_weight), transposed_right(grad_delta, attn_weight)], 1
    )
    grad_mixed = grad_mixed.astype(jnp.bfloat16).astype(jnp.float32)
    (
        grad_inner_gate,
        grad_state_in,
        raw_step_gradient,
        grad_query_in,
        grad_keyval_in,
        grad_conv_inner,
        conv_state_gradient,
        grad_step_bias,
        grad_decay_log,
        grad_skip_gain,
    ) = mixer_pull(grad_mixed)
    grad_state_in, conv_state_gradient = (
        lax.psum(grad_state_in.astype(jnp.bfloat16), "col").astype(jnp.float32),
        lax.psum(conv_state_gradient.astype(jnp.bfloat16), "col").astype(jnp.float32),
    )
    round_inner = grad_inner_gate.astype(jnp.bfloat16)
    round_state = grad_state_in.astype(jnp.bfloat16)
    round_step = raw_step_gradient.astype(jnp.bfloat16)
    round_query = grad_query_in.astype(jnp.bfloat16)
    round_keyval = grad_keyval_in.astype(jnp.bfloat16)
    grad_inner_weight = transposed_left(normed, round_inner).reshape(model_width, 2, -1)
    grad_state_weight = transposed_left(normed, round_state)
    grad_step_weight = transposed_left(normed, round_step)
    grad_query_weight = transposed_left(normed, round_query)
    grad_keyval_weight = transposed_left(normed, round_keyval).reshape(model_width, 2, -1)
    own_heads = (
        transposed_right(round_inner, inner_weight.reshape(model_width, -1))
        + transposed_right(round_step, step_weight)
        + transposed_right(round_query, query_weight)
        + transposed_right(round_keyval, keyval_weight.reshape(model_width, -1))
    )
    grad_normed = normed_total(own_heads) + transposed_right(round_state, state_weight)
    back_hidden, grad_gain_mixer = norm_back(hidden, gain_mixer.astype(jnp.float32), grad_normed)
    input_grad = grad_middle + back_hidden
    (
        grad_mixer_gain,
        grad_ssm_inner,
        grad_state_proj,
        grad_step_proj,
        grad_query_proj,
        grad_keyval_proj,
        grad_ffn_gain,
        grad_gate_up,
    ) = (
        lax.psum_scatter(grad_gain_mixer, ("dp", "row"), scatter_dimension=0, tiled=True),
        lax.psum_scatter(grad_inner_weight, ("dp", "row"), scatter_dimension=0, tiled=True),
        lax.psum_scatter(grad_state_weight, ("dp", "row"), scatter_dimension=0, tiled=True),
        lax.psum_scatter(grad_step_weight, ("dp", "row"), scatter_dimension=0, tiled=True),
        lax.psum_scatter(grad_query_weight, ("dp", "row"), scatter_dimension=0, tiled=True),
        lax.psum_scatter(grad_keyval_weight, ("dp", "row"), scatter_dimension=0, tiled=True),
        lax.psum_scatter(grad_gain_ffn, ("dp", "row"), scatter_dimension=0, tiled=True),
        lax.psum_scatter(
            grad_gate_weight.reshape(model_width, 2, -1),
            ("dp", "row"),
            scatter_dimension=0,
            tiled=True,
        ),
    )
    grad_ssm_out, grad_attn_out, grad_down_proj = (
        lax.psum_scatter(grad_ssm_weight, ("dp", "row"), scatter_dimension=1, tiled=True),
        lax.psum_scatter(grad_attn_weight, ("dp", "row"), scatter_dimension=1, tiled=True),
        lax.psum_scatter(grad_down, ("dp", "row"), scatter_dimension=1, tiled=True),
    )
    grad_conv_inner, conv_state_gradient, grad_step_bias, grad_decay_log, grad_skip_gain = lax.psum(
        (grad_conv_inner, conv_state_gradient, grad_step_bias, grad_decay_log, grad_skip_gain),
        ("dp", "row"),
    )
    return (
        hidden_out,
        input_grad,
        grad_mixer_gain,
        grad_ssm_inner,
        grad_state_proj,
        grad_step_proj,
        grad_query_proj,
        grad_keyval_proj,
        grad_conv_inner,
        conv_state_gradient,
        grad_step_bias,
        grad_decay_log,
        grad_skip_gain,
        grad_ssm_out,
        grad_attn_out,
        grad_ffn_gain,
        grad_gate_up,
        grad_down_proj,
    )


def solution(mesh):
    placed = (
        P(("dp", "row"), None),
        P(("dp", "row")),
        P(("dp", "row")),
        P(("dp", "row"), None, "col"),
        P(("dp", "row"), None),
        P(("dp", "row"), "col"),
        P(("dp", "row"), "col"),
        P(("dp", "row"), None, "col"),
        P(None, "col"),
        P(),
        P("col"),
        P("col"),
        P("col"),
        P("col", ("dp", "row")),
        P("col", ("dp", "row")),
        P(("dp", "row")),
        P(("dp", "row"), None, "col"),
        P("col", ("dp", "row")),
        P(("dp", "row"), None),
    )
    return jax.shard_map(
        local,
        mesh=mesh,
        in_specs=placed,
        out_specs=(
            P(("dp", "row"), None),
            P(("dp", "row"), None),
            P(("dp", "row")),
            P(("dp", "row"), None, "col"),
            P(("dp", "row"), None),
            P(("dp", "row"), "col"),
            P(("dp", "row"), "col"),
            P(("dp", "row"), None, "col"),
            P(None, "col"),
            P(),
            P("col"),
            P("col"),
            P("col"),
            P("col", ("dp", "row")),
            P("col", ("dp", "row")),
            P(("dp", "row")),
            P(("dp", "row"), None, "col"),
            P("col", ("dp", "row")),
        ),
        check_vma=False,
    )
```

profile of v0, /device:TPU:0, one launch (start us, length us, event | category | flops | bytes accessed | tf_op | source)
XLA Modules:
  0.0 2399.3 jit_solution(1090059003909030930)
XLA Ops:
  14.4 44.6 %all-reduce.40 = (bf16[1024]{0:T(1024)(128)(2,1)S(1)}, bf16[1024]{0:T(1024)(128)(2,1)}) all-reduce(bf16[1024]{0:T(1024)(128)(2,1)S(1)} %dynamic-update-slice.14, bf16[1024]{0:T(1024)(128)(2,1)S(1)} %dynamic-update-slice.15), channel_id=1, replica_groups=mesh['dp'=4,'row'=4,'col'=2] {'dp','row'}, use_global_device_ids=true, to_apply=%add.34 | all-reduce | flops 2048 | bytes 8192
  62.6 40.6 %all_gather.47 = bf16[1024,256]{1,0:T(8,128)(2,1)S(1)} all-gather(bf16[64,256]{1,0:T(8,128)(2,1)} %param.33), channel_id=1, replica_groups=mesh['dp'=4,'row'=4,'col'=2] {'dp','row'}, dimensions={0}, use_global_device_ids=true | all-gather | bytes 557056 | tf_op jit(solution)/shard_map/all_gather | solution.py:225
  112.7 37.4 %all-gather = bf16[16,64,12]{1,2,0:T(8,128)(2,1)S(1)} all-gather(bf16[1,64,12]{1,2,0:T(8,128)(2,1)S(1)} %bitcast.1043), channel_id=1, replica_groups=mesh['dp'=4,'row'=4,'col'=2] {'dp','row'}, dimensions={0}, use_global_device_ids=true | all-gather | bytes 26112 | tf_op jit(solution)/shard_map/all_gather | solution.py:226
  157.9 41.7 %all_gather.48 = bf16[1024,256]{1,0:T(8,128)(2,1)S(1)} all-gather(bf16[64,256]{1,0:T(8,128)(2,1)} %param.35), channel_id=1, replica_groups=mesh['dp'=4,'row'=4,'col'=2] {'dp','row'}, dimensions={0}, use_global_device_ids=true | all-gather | bytes 557056 | tf_op jit(solution)/shard_map/all_gather | solution.py:227
  201.9 44.2 %all_gather.49 = bf16[1024,2,64]{2,1,0:T(2,128)(2,1)} all-gather(bf16[64,2,64]{2,1,0:T(2,128)(2,1)S(1)} %copy-done.112), channel_id=1, replica_groups=mesh['dp'=4,'row'=4,'col'=2] {'dp','row'}, dimensions={0}, use_global_device_ids=true | all-gather | bytes 278528 | tf_op jit(solution)/shard_map/all_gather | solution.py:228
  250.6 58.0 %while.119 = (s32[]{:T(128)}, bf16[2,1,512,1,4,64]{2,5,4,3,1,0:T(8,128)(2,1)}, s32[2]{0:T(128)}, s32[1,1024]{1,0:T(1,128)}, s32[1,1,1024]{2,1,0:T(1,128)}, /*ind...) while((s32[]{:T(128)}, ...), condition=%wide.region_8.9_spmd.clone, body=%wide.region_5.8_spmd.clone.sunk | while | flops 3245863424 | bytes 29940980 | solution.py:123
  313.9 42.6 %all_gather.51 = bf16[256,1024]{0,1:T(8,128)(2,1)} all-gather(bf16[256,64]{0,1:T(8,128)(2,1)} %param.43), channel_id=1, replica_groups=mesh['dp'=4,'row'=4,'col'=2] {'dp','row'}, dimensions={1}, use_global_device_ids=true | all-gather | bytes 557056 | tf_op jit(solution)/shard_map/all_gather | solution.py:234
  386.1 307.5 %while.120 = (s32[]{:T(128)}, f32[1,12,64,128]{3,2,1,0:T(8,128)S(1)}, f32[4,1,256,12,64]{2,0,4,3,1:T(4,128)}, f32[4,1,256,256,12]{3,2,4,1,0:T(8,128)}, f32[4,1,2...) while((s32[]{:T(128)}, ...), condition=%wide.region_4.5_spmd.clone, body=%wide.region_1.4_spmd.clone.sunk | while | flops 1321518080 | bytes 32232148 | solution.py:71
  424.3 17.9 dynamic_update_slice.264
  501.2 17.9 dynamic_update_slice.264
  578.0 17.9 dynamic_update_slice.264
  654.8 17.9 dynamic_update_slice.264
  743.8 52.7 %all-gather.12.cloned.1.call-done = bf16[1024,1024]{0,1:T(8,128)(2,1)} async-done(((bf16[1024,64]{0,1:T(8,128)(2,1)}), bf16[1024,1024]{0,1:T(8,128)(2,1)}) %all-gather.12.cloned.1.call-update) | async-done | bytes 2097168 | tf_op jit(solution)/shard_map/all_gather | solution.py:235
  820.6 21.2 all-reduce.50.cloned.1.call-done
  873.4 255.9 %while.121 = (s32[]{:T(128)}, f32[1,12,64,128]{3,2,1,0:T(8,128)S(1)}, f32[4,1,256,12,64]{2,0,4,3,1:T(4,128)}, f32[4,1,256,128]{3,2,1,0:T(8,128)}, f32[4,1,256,12...) while((s32[]{:T(128)}, ...), condition=%wide.region_24.25_spmd.clone, body=%wide.region_14.24_spmd.clone.sunk | while | flops 2628688896 | bytes 43313328 | solution.py:71
  907.0 17.9 dynamic_update_slice.274
  970.8 17.9 dynamic_update_slice.274
  1034.7 17.9 dynamic_update_slice.274
  1098.5 17.9 dynamic_update_slice.274
  1146.7 178.9 %while.122 = (s32[]{:T(128)}, f32[1,1024,1,4,64]{1,4,3,2,0:T(8,128)}, f32[1,1024,1,64]{1,3,2,0:T(8,128)}, f32[1,1024,1,64]{1,3,2,0:T(8,128)}, s32[2]{0:T(128)}, ...) while((s32[]{:T(128)}, ...), condition=%wide.region_32.33_spmd.clone, body=%wide.region_25.32_spmd.clone.sunk | while | flops 8128561664 | bytes 180297264 | solution.py:123
  1202.5 13.2 convert_reduce_fusion.2
  1277.4 13.2 convert_reduce_fusion.2
  1447.6 38.2 %reduce-scatter.17.cloned.1.call-done = f32[64,2,64]{2,0,1:T(8,128)} async-done(((f32[1024,2,64]{2,0,1:T(8,128)}), f32[64,2,64]{2,0,1:T(8,128)}) %reduce-scatter.17.cloned.1.call-update) | async-done | bytes 32784 | tf_op jit(solution)/shard_map/reduce_scatter | solution.py:422
  1487.3 258.2 %all-reduce.54.cloned.1.call-done = f32[1024,2,1024]{2,1,0:T(2,128)} async-done(((f32[1024,2,1024]{2,1,0:T(2,128)}), f32[1024,2,1024]{2,1,0:T(2,128)}) %all-reduce.54.cloned.1.call-update) | async-done | bytes 8388624
  1747.4 28.7 %all-reduce.52.cloned.1.call-done = f32[1024,1024]{1,0:T(8,128)} async-done(((f32[1024,1024]{1,0:T(8,128)}), f32[1024,1024]{1,0:T(8,128)}) %all-reduce.52.cloned.1.call-update) | async-done | bytes 4194320 | tf_op jit(solution)/shard_map/psum | solution.py:198
  1781.7 77.9 %all-reduce.39 = (f32[1024]{0:T(1024)S(1)}, f32[4,768]{1,0:T(4,128)}, f32[4,256]{1,0:T(4,128)}, f32[12]{0:T(128)}, f32[12]{0:T(128)}, /*index=5*/f32[12]{0:T(128)}, f32[1024]{0:T(1024)S(1)}) all-reduce(f32[1024]{0:T(1024)S(1)} %get-tuple-element.2207, ...), channel_id=2, replica_groups=mesh['dp'=4,'row'=4,'col'=2] {'dp','row'}, use_global_device_ids=true, to_apply=%region_37.38.clone | all-reduce | flops 6180 | bytes 47392
  1869.2 59.0 %reduce-scatter.11.cloned.1.call-done = f32[64,2,768]{2,0,1:T(8,128)} async-done(((f32[1024,2,768]{2,0,1:T(8,128)}), f32[64,2,768]{2,0,1:T(8,128)}) %reduce-scatter.11.cloned.1.call-update) | async-done | bytes 393232 | tf_op jit(solution)/shard_map/reduce_scatter | solution.py:418
  1930.3 77.6 %reduce-scatter.21.cloned.1.call-done = f32[256,64]{0,1:T(8,128)} async-done(((f32[256,1024]{0,1:T(8,128)}), f32[256,64]{0,1:T(8,128)}) %reduce-scatter.21.cloned.1.call-update) | async-done | bytes 65552 | tf_op jit(solution)/shard_map/reduce_scatter | solution.py:433
  2007.8 76.8 %reduce-scatter.15.cloned.1.call-done = f32[64,256]{1,0:T(8,128)} async-done(((f32[1024,256]{1,0:T(8,128)}), f32[64,256]{1,0:T(8,128)}) %reduce-scatter.15.cloned.1.call-update) | async-done | bytes 65552 | tf_op jit(solution)/shard_map/reduce_scatter | solution.py:421
  2084.7 94.2 %reduce-scatter.23.cloned.1.call-done = f32[1024,64]{0,1:T(8,128)} async-done(((f32[1024,1024]{0,1:T(8,128)}), f32[1024,64]{0,1:T(8,128)}) %reduce-scatter.23.cloned.1.call-update) | async-done | bytes 262160 | tf_op jit(solution)/shard_map/reduce_scatter | solution.py:434
  2178.9 80.0 %reduce-scatter.13.cloned.1.call-done = f32[64,256]{1,0:T(8,128)} async-done(((f32[1024,256]{1,0:T(8,128)}), f32[64,256]{1,0:T(8,128)}) %reduce-scatter.13.cloned.1.call-update) | async-done | bytes 65552 | tf_op jit(solution)/shard_map/reduce_scatter | solution.py:419
  2258.9 133.3 %reduce-scatter.19.cloned.1.call-done = f32[768,64]{0,1:T(8,128)} async-done(((f32[768,1024]{0,1:T(8,128)}), f32[768,64]{0,1:T(8,128)}) %reduce-scatter.19.cloned.1.call-update) | async-done | bytes 196624 | tf_op jit(solution)/shard_map/reduce_scatter | solution.py:432
  (986 shorter events, 918.8 us)
Async XLA Ops:
  7.2 351.1 %all-gather.6.cloned.1.call-start = ((), (), s32[]{:S(2)}) async-start(), calls=%async_computation.8 | async-start | bytes 3342336 | tf_op jit(solution)/shard_map/all_gather | solution.py:224
  7.9 700.1 %all-gather.8.cloned.1.call-start = ((), (), s32[]{:S(2)}) async-start(), calls=%async_computation.9 | async-start | bytes 1671168 | tf_op jit(solution)/shard_map/all_gather | solution.py:233
  8.7 706.3 %all-gather.10.cloned.1.call-start = ((), (), s32[]{:S(2)}) async-start(), calls=%async_computation.11 | async-start | bytes 4456448 | tf_op jit(solution)/shard_map/all_gather | solution.py:230
  9.4 722.2 %all-reduce.48.cloned.1.call-start = ((), (), s32[]{:S(2)}) async-start(), calls=%async_computation.10 | async-start | bytes 4194304 | tf_op jit(solution)/shard_map/psum | solution.py:194
  62.6 302.5 %copy-start.104 = (f32[768]{0:T(1024)}, f32[768]{0:T(1024)S(1)}, u32[]{:S(2)}) copy-start(f32[768]{0:T(1024)S(1)} %get-tuple-element.2211) | copy-start | bytes 9220
  107.9 257.2 %copy-start.78 = (f32[1,1024]{1,0:T(1,128)}, f32[1,1024]{1,0:T(1,128)S(1)}, u32[]{:S(2)}) copy-start(f32[1,1024]{1,0:T(1,128)S(1)} %get-tuple-element.2495) | copy-start | bytes 12292
  107.9 257.2 %copy-start.84 = (f32[1,1024]{1,0:T(1,128)}, f32[1,1024]{1,0:T(1,128)S(1)}, u32[]{:S(2)}) copy-start(f32[1,1024]{1,0:T(1,128)S(1)} %get-tuple-element.2496) | copy-start | bytes 12292
  108.7 256.4 %copy-start.81 = (f32[1024]{0:T(1024)}, f32[1024]{0:T(1024)S(1)}, u32[]{:S(2)}) copy-start(f32[1024]{0:T(1024)S(1)} %fusion.290) | copy-start | bytes 12292
  714.3 82.3 %all-gather.12.cloned.1.call-start = ((), (), s32[]{:S(2)}) async-start(), calls=%async_computation.12 | async-start | bytes 2228224 | tf_op jit(solution)/shard_map/all_gather | solution.py:235
  714.9 126.9 %all-reduce.50.cloned.1.call-start = ((), (), s32[]{:S(2)}) async-start(), calls=%async_computation.13 | async-start | bytes 8388608 | tf_op jit(solution)/shard_map/psum | solution.py:198
  714.9 131.9 %copy-start.87 = (f32[1024]{0:T(1024)}, f32[1024]{0:T(1024)S(1)}, u32[]{:S(2)}) copy-start(f32[1024]{0:T(1024)S(1)} %convert_element_type.188) | copy-start | bytes 12292
  814.6 618.6 %all-reduce.56.cloned.1.call-start = ((), (), s32[]{:S(2)}) async-start(), calls=%async_computation.24 | async-start | bytes 5242880 | tf_op jit(solution)/shard_map/psum | solution.py:194
  873.4 255.9 %copy-start.11 = (f32[1024,256]{1,0:T(8,128)S(1)}, f32[1024,256]{1,0:T(8,128)}, u32[]{:S(2)}) copy-start(f32[1024,256]{1,0:T(8,128)} %copy-done.10) | copy-start | bytes 3145732
  873.4 255.9 %copy-start.85 = (f32[1,1024]{1,0:T(1,128)S(1)}, f32[1,1024]{1,0:T(1,128)}, u32[]{:S(2)}) copy-start(f32[1,1024]{1,0:T(1,128)} %copy-done.84) | copy-start | bytes 12292
  1145.5 300.6 %reduce-scatter.25.cloned.1.call-start = ((), (), s32[]{:S(2)}) async-start(), calls=%async_computation.22 | async-start | bytes 557056
  1146.7 179.0 %copy-start.76 = (f32[4,1,256,12]{2,0,3,1:T(4,128)S(1)}, f32[4,1,256,12]{2,0,3,1:T(4,128)}, u32[]{:S(2)}) copy-start(f32[4,1,256,12]{2,0,3,1:T(4,128)} %copy-done.75) | copy-start | bytes 147460
  1146.7 182.4 %copy-start.69 = (f32[1024,12]{0,1:T(8,128)S(1)}, f32[1024,12]{0,1:T(8,128)}, u32[]{:S(2)}) copy-start(f32[1024,12]{0,1:T(8,128)} %get-tuple-element.2501) | copy-start | bytes 147460
  1146.7 183.3 %copy-start.8 = (bf16[1024,1024]{1,0:T(8,128)(2,1)S(1)}, bf16[1024,1024]{1,0:T(8,128)(2,1)}, u32[]{:S(2)}) copy-start(bf16[1024,1024]{1,0:T(8,128)(2,1)} %copy-done.6) | copy-start | bytes 6291460
  1331.5 154.3 %reduce-scatter.17.cloned.1.call-start = ((), (), s32[]{:S(2)}) async-start(), calls=%async_computation.18 | async-start | bytes 1114112 | tf_op jit(solution)/shard_map/reduce_scatter | solution.py:422
  1335.1 410.3 %all-reduce.54.cloned.1.call-start = ((), (), s32[]{:S(2)}) async-start(), calls=%async_computation.23 | async-start | bytes 16777216
  1358.1 418.0 %all-reduce.52.cloned.1.call-start = ((), (), s32[]{:S(2)}) async-start(), calls=%async_computation.14 | async-start | bytes 8388608 | tf_op jit(solution)/shard_map/psum | solution.py:198
  1400.7 527.5 %reduce-scatter.11.cloned.1.call-start = ((), (), s32[]{:S(2)}) async-start(), calls=%async_computation.15 | async-start | bytes 6684672 | tf_op jit(solution)/shard_map/reduce_scatter | solution.py:418
  1419.2 588.7 %reduce-scatter.21.cloned.1.call-start = ((), (), s32[]{:S(2)}) async-start(), calls=%async_computation.20 | async-start | bytes 1114112 | tf_op jit(solution)/shard_map/reduce_scatter | solution.py:433
  1422.9 661.7 %reduce-scatter.15.cloned.1.call-start = ((), (), s32[]{:S(2)}) async-start(), calls=%async_computation.17 | async-start | bytes 1114112 | tf_op jit(solution)/shard_map/reduce_scatter | solution.py:421
  1426.3 752.6 %reduce-scatter.23.cloned.1.call-start = ((), (), s32[]{:S(2)}) async-start(), calls=%async_computation.21 | async-start | bytes 4456448 | tf_op jit(solution)/shard_map/reduce_scatter | solution.py:434
  1433.1 825.9 %reduce-scatter.13.cloned.1.call-start = ((), (), s32[]{:S(2)}) async-start(), calls=%async_computation.16 | async-start | bytes 1114112 | tf_op jit(solution)/shard_map/reduce_scatter | solution.py:419
  1436.6 955.7 %reduce-scatter.19.cloned.1.call-start = ((), (), s32[]{:S(2)}) async-start(), calls=%async_computation.19 | async-start | bytes 3342336 | tf_op jit(solution)/shard_map/reduce_scatter | solution.py:432
  1442.2 333.9 %copy-start.55 = (bf16[1024,256]{1,0:T(8,128)(2,1)S(1)}, bf16[1024,256]{1,0:T(8,128)(2,1)}, u32[]{:S(2)}) copy-start(bf16[1024,256]{1,0:T(8,128)(2,1)} %copy-done.54) | copy-start | bytes 1572868
  1442.2 333.9 %copy-start.66 = (bf16[1024,256]{1,0:T(8,128)(2,1)S(1)}, bf16[1024,256]{1,0:T(8,128)(2,1)}, u32[]{:S(2)}) copy-start(bf16[1024,256]{1,0:T(8,128)(2,1)} %get-tuple-element.2391) | copy-start | bytes 1572868
  1442.2 333.9 %copy-start.92 = (f32[1024]{0:T(1024)S(1)}, f32[1024]{0:T(1024)}, u32[]{:S(2)}) copy-start(f32[1024]{0:T(1024)} %copy-done.91) | copy-start | bytes 12292
  1442.3 333.9 %copy-start.94 = (f32[1024]{0:T(1024)S(1)}, f32[1024]{0:T(1024)}, u32[]{:S(2)}) copy-start(f32[1024]{0:T(1024)} %copy-done.93) | copy-start | bytes 12292
  1747.4 113.4 %copy-start.101 = (f32[1024]{0:T(1024)S(1)}, f32[1024]{0:T(1024)}, u32[]{:S(2)}) copy-start(f32[1024]{0:T(1024)} %copy-done.100) | copy-start | bytes 12292
  (176 other events, 1848.8 us)
Sparse Core Ops, SparseCore 0:
  10.8 75.9 all-gather.5
  89.6 58.4 all-gather.7
  150.9 81.4 all-gather.9
  714.4 17.2 all-reduce.47
  734.6 61.8 all-gather.11
  814.7 27.0 all-reduce.49
  1145.6 23.3 all-reduce.55
  1331.7 77.8 reduce-scatter.24
  1411.8 73.9 reduce-scatter.16
  1492.7 252.7 all-reduce.53
  1748.7 27.3 all-reduce.51
  1781.2 146.9 reduce-scatter.10
  1931.0 76.7 reduce-scatter.20
  2010.6 74.0 reduce-scatter.14
  2087.4 91.4 reduce-scatter.22
  2181.6 77.2 reduce-scatter.12
  2265.1 127.1 reduce-scatter.18
where the time goes:
time: 2420 us; the launch traced here: 2400 us
  waiting for transfers between devices  933 us (39%)
  local copies, waits for them, and re-layouts  437 us (18%)
  matrix products  408 us (17%)
  blocking collectives  332 us (14%)
  other arithmetic  228 us (9%)
  loops' own time  44.3 us (2%)
    unnamed x19, waiting for transfers between devices  261 us
    dynamic_update_slice x72, local copies, waits for them, and re-layouts, state_scan(): lax.scan(advance, initial, (inner_blocks, input_blocks, output_blocks, st...  224 us
    reduce_scatter x1, waiting for transfers between devices, local(): lax.psum_scatter(grad_ssm_weight, ('dp', 'row'), scatter_dimension=1, til...  133 us
    unnamed x2, blocking collectives  123 us
    reduce_scatter x1, waiting for transfers between devices, local(): lax.psum_scatter(grad_down, ('dp', 'row'), scatter_dimension=1, tiled=True)  94.2 us
    reduce_scatter x1, waiting for transfers between devices, local(): lax.psum_scatter(grad_state_weight, ('dp', 'row'), scatter_dimension=0, t...  80 us
    reduce_scatter x1, waiting for transfers between devices, local(): lax.psum_scatter(grad_attn_weight, ('dp', 'row'), scatter_dimension=1, ti...  77.6 us
    reduce_scatter x1, waiting for transfers between devices, local(): lax.psum_scatter(grad_query_weight, ('dp', 'row'), scatter_dimension=0, t...  76.8 us
  transfers between devices with their start and end apart: 17, of which 12 were waited for; matrix products, arithmetic and copies ran while one was open for 31% of the time, Pallas kernels for 0%

commit v1 on v0

v1 whole, which is shorter than its diff:
```python
import jax
import jax.numpy as jnp
from jax import lax
from jax.experimental import pallas as pl
from jax.experimental.pallas import tpu as pltpu
from jax.sharding import PartitionSpec as P

HEAD_SIZE = 64
SEQ_LEN = 1024
SPAN = 256


EPS = 1e-05
THETA = 100000000000.0
HIGH = lax.Precision.HIGHEST


def causal_conv(signal, kernel, segment_ids):
    length = signal.shape[0]
    kernel_width = kernel.shape[0]
    summed = signal * kernel[kernel_width - 1][None, :]
    for offset in range(1, kernel_width):
        shifted = jnp.concatenate(
            [jnp.zeros((offset, signal.shape[1]), signal.dtype), signal[: length - offset]], 0
        )
        earlier = jnp.concatenate(
            [jnp.full((offset,), -1, segment_ids.dtype), segment_ids[: length - offset]], 0
        )
        matches = (earlier == segment_ids).astype(signal.dtype)
        summed = summed + shifted * kernel[kernel_width - 1 - offset][None, :] * matches[:, None]
    return summed


def contract(left, right, left_dim, right_dim):
    return lax.dot_general(
        left.astype(jnp.bfloat16),
        right.astype(jnp.bfloat16),
        (((left_dim,), (right_dim,)), ((), ())),
        preferred_element_type=jnp.float32,
    )


def plain_nn(left, right):
    return contract(left, right, 1, 0)


def plain_nt(left, right):
    return contract(left, right, 1, 1)


def plain_tn(left, right):
    return contract(left, right, 0, 0)


def with_back(forward, back):
    wrapped = jax.custom_vjp(forward)
    wrapped.defvjp(lambda left, right: (forward(left, right), (left, right)), back)
    return wrapped


PLAIN = (plain_nn, plain_nt, plain_tn)
BACKED = (
    with_back(plain_nn, lambda kept, g: (plain_nt(g, kept[1]), plain_tn(kept[0], g))),
    with_back(plain_nt, lambda kept, g: (plain_nn(g, kept[1]), plain_tn(g, kept[0]))),
    with_back(plain_tn, lambda kept, g: (plain_nt(kept[1], g), plain_nn(kept[0], g))),
)
PAIR = 2
COLUMN_KINDS = 4
LANES = 128
VMEM_BYTES = 48 * 1024 * 1024


def causal_mask(segment_column, segment_row, row_start):
    shape = (segment_column.shape[0], segment_row.shape[1])
    rows = lax.broadcasted_iota(jnp.int32, shape, 0) + row_start
    columns = lax.broadcasted_iota(jnp.int32, shape, 1)
    return (segment_column == segment_row) & (rows >= columns)


def scan_math(pieces, masks, dots):
    product, product_right, product_left = dots
    inner, input_map, output_map, running, step, entering, leaving, running_row, keeping = pieces
    blocks = len(masks)
    outputs = [[None] * blocks for _ in range(PAIR)]
    carried = [None] * PAIR
    for block in range(blocks):
        intersection = product_right(output_map[block], input_map[block])
        for head in range(PAIR):
            part = inner[head][block]
            spread = running[head][block] - running_row[head][block]
            decay = jnp.exp(jnp.where(masks[block], spread, -1e30))
            result = product(decay * intersection, part * step[head][block])
            if block:
                result = result + (
                    product_right(output_map[block], carried[head]) * entering[head][block]
                )
            outputs[head][block] = result
            if block < blocks - 1:
                added = product_left(part * leaving[head][block], input_map[block])
                carried[head] = (
                    carried[head] * keeping[head][block] + added if block else added
                )
    return outputs


def scan_pieces(inner, input_map, output_map, columns, rows, segment_column, segment_row):
    blocks = inner.shape[0] // SPAN
    spans = [slice(SPAN * block, SPAN * (block + 1)) for block in range(blocks)]
    heads = range(PAIR)

    def column(kind):
        return [
            [columns[0, span, kind * PAIR + head : kind * PAIR + head + 1] for span in spans]
            for head in heads
        ]

    pieces = (
        [[inner[span, HEAD_SIZE * head : HEAD_SIZE * (head + 1)] for span in spans] for head in heads],
        [input_map[span, :] for span in spans],
        [output_map[span, :] for span in spans],
        column(0),
        column(1),
        column(2),
        column(3),
        [[rows[0, head : head + 1, span] for span in spans] for head in heads],
        [
            [rows[0, PAIR + head : PAIR + head + 1, span.start : span.start + LANES] for span in spans]
            for head in heads
        ],
    )
    masks = [causal_mask(segment_column[span, :], segment_row[:, span], 0) for span in spans]
    return pieces, masks, spans


def scan_forward_kernel(inner, input_map, output_map, columns, rows, seg_col, seg_row, out):
    pieces, masks, spans = scan_pieces(
        inner, input_map, output_map, columns, rows, seg_col, seg_row
    )
    results = scan_math(pieces, masks, PLAIN)
    for head in range(PAIR):
        for block, span in enumerate(spans):
            out[span, HEAD_SIZE * head : HEAD_SIZE * (head + 1)] = results[head][block]


def scan_backward_kernel(
    inner, input_map, output_map, columns, rows, seg_col, seg_row, cotangent,
    inner_grad, input_map_grad, output_map_grad, column_grad, row_grad,
):
    pieces, masks, spans = scan_pieces(
        inner, input_map, output_map, columns, rows, seg_col, seg_row
    )
    _, pullback = jax.vjp(lambda held: scan_math(held, masks, BACKED), pieces)
    (grads,) = pullback(
        [
            [cotangent[span, HEAD_SIZE * head : HEAD_SIZE * (head + 1)] for span in spans]
            for head in range(PAIR)
        ]
    )

    @pl.when(pl.program_id(0) == 0)
    def _():
        input_map_grad[...] = jnp.zeros_like(input_map_grad)
        output_map_grad[...] = jnp.zeros_like(output_map_grad)

    row_grad[...] = jnp.zeros_like(row_grad)
    for block, span in enumerate(spans):
        input_map_grad[span, :] += grads[1][block]
        output_map_grad[span, :] += grads[2][block]
        for head in range(PAIR):
            inner_grad[span, HEAD_SIZE * head : HEAD_SIZE * (head + 1)] = grads[0][head][block]
            for kind in range(COLUMN_KINDS):
                at = kind * PAIR + head
                column_grad[0, span, at : at + 1] = grads[3 + kind][head][block]
            row_grad[0, head : head + 1, span] = grads[7][head][block]
            row_grad[0, PAIR + head : PAIR + head + 1, span.start : span.start + LANES] = grads[8][
                head
            ][block]


def whole(array):
    return pl.BlockSpec(array.shape, lambda pair: (0,) * array.ndim)


def scan_specs(inner, input_map, output_map, columns, rows, seg_col, seg_row):
    return [
        pl.BlockSpec((inner.shape[0], PAIR * HEAD_SIZE), lambda pair: (0, pair)),
        whole(input_map),
        whole(output_map),
        pl.BlockSpec((1,) + columns.shape[1:], lambda pair: (pair, 0, 0)),
        pl.BlockSpec((1,) + rows.shape[1:], lambda pair: (pair, 0, 0)),
        whole(seg_col),
        whole(seg_row),
    ]


def run_kernel(body, operands, in_specs, outs, out_specs, grid, flops):
    return pl.pallas_call(
        body,
        grid=(grid,),
        in_specs=in_specs,
        out_specs=out_specs,
        out_shape=[jax.ShapeDtypeStruct(out.shape, jnp.float32) for out in outs],
        compiler_params=pltpu.CompilerParams(vmem_limit_bytes=VMEM_BYTES),
        cost_estimate=pl.CostEstimate(
            flops=flops, bytes_accessed=64 * 1024 * 1024, transcendentals=0
        ),
    )(*operands)


@jax.custom_vjp
def pair_scan(*operands):
    specs = scan_specs(*operands)
    return run_kernel(
        scan_forward_kernel,
        operands,
        specs,
        [operands[0]],
        [specs[0]],
        operands[3].shape[0],
        10**10,
    )[0]


def pair_scan_back(operands, cotangent):
    specs = scan_specs(*operands)
    grads = run_kernel(
        scan_backward_kernel,
        operands + (cotangent,),
        specs + [specs[0]],
        operands[:5],
        specs[:5],
        operands[3].shape[0],
        3 * 10**10,
    )
    return tuple(grads) + (jnp.zeros_like(operands[5]), jnp.zeros_like(operands[6]))


pair_scan.defvjp(lambda *operands: (pair_scan(*operands), operands), pair_scan_back)


def scan_columns(step_size, decay_rate, segments):
    length, heads = step_size.shape
    blocks = length // SPAN
    decay_blocks = (step_size * decay_rate[None, :]).reshape(blocks, SPAN, heads)
    lower = jnp.tril(jnp.ones((SPAN, SPAN), jnp.float32))
    running = jnp.einsum("ts,bsh->bth", lower, decay_blocks, precision=HIGH)
    last = running[:, -1:, :]
    segment_blocks = segments.reshape(blocks, SPAN)
    final = segment_blocks[:, -1]
    before = jnp.concatenate([segment_blocks[0, :1], final[:-1]], 0)
    enters = (segment_blocks == before[:, None]).astype(jnp.float32)[:, :, None]
    leaves = (segment_blocks == final[:, None]).astype(jnp.float32)[:, :, None]
    keeps = (final == before).astype(jnp.float32)[:, None, None]
    entering = (enters * jnp.exp(running)).reshape(length, heads)
    leaving = (leaves * jnp.exp(last - running)).reshape(length, heads) * step_size
    keeping = jnp.broadcast_to(keeps * jnp.exp(last), running.shape).reshape(length, heads)
    running = running.reshape(length, heads)
    pairs = heads // PAIR
    columns = jnp.stack([running, step_size, entering, leaving], 0)
    columns = columns.reshape(COLUMN_KINDS, length, pairs, PAIR).transpose(2, 1, 0, 3)
    rows = jnp.stack([running.T, keeping.T], 0).reshape(2, pairs, PAIR, length)
    rows = rows.transpose(1, 0, 2, 3).reshape(pairs, 2 * PAIR, length)
    return columns.reshape(pairs, length, COLUMN_KINDS * PAIR), rows


def attend_math(queries, keys_in, values_in, mask, dots):
    scores = jnp.where(mask, dots[1](queries, keys_in), -1e30)
    highest = lax.stop_gradient(jnp.max(scores, axis=-1, keepdims=True))
    weights = jnp.exp(scores - highest)
    total = jnp.sum(weights, axis=-1, keepdims=True)
    return dots[0](weights, values_in) / total


def attend_blocks(queries, seg_col, seg_row):
    for start in range(0, queries.shape[0], SPAN):
        rows = slice(start, start + SPAN)
        keys = slice(0, start + SPAN)
        mask = causal_mask(seg_col[rows, :], seg_row[:, keys], start)
        for head in range(PAIR):
            yield rows, keys, slice(HEAD_SIZE * head, HEAD_SIZE * (head + 1)), mask


def attend_forward_kernel(queries, keys_in, values_in, seg_col, seg_row, out):
    for rows, keys, lanes, mask in attend_blocks(queries, seg_col, seg_row):
        out[rows, lanes] = attend_math(
            queries[rows, lanes], keys_in[keys, :], values_in[keys, :], mask, PLAIN
        )


def attend_backward_kernel(
    queries, keys_in, values_in, seg_col, seg_row, cotangent, query_grad, key_grad, value_grad
):
    @pl.when(pl.program_id(0) == 0)
    def _():
        key_grad[...] = jnp.zeros_like(key_grad)
        value_grad[...] = jnp.zeros_like(value_grad)

    for rows, keys, lanes, mask in attend_blocks(queries, seg_col, seg_row):
        _, pullback = jax.vjp(
            lambda q, k, v: attend_math(q, k, v, mask, BACKED),
            queries[rows, lanes],
            keys_in[keys, :],
            values_in[keys, :],
        )
        query_part, key_part, value_part = pullback(cotangent[rows, lanes])
        query_grad[rows, lanes] = query_part
        key_grad[keys, :] += key_part
        value_grad[keys, :] += value_part


def attend_specs(queries, keys_in, values_in, seg_col, seg_row):
    return [
        pl.BlockSpec((queries.shape[0], PAIR * HEAD_SIZE), lambda pair: (0, pair)),
        whole(keys_in),
        whole(values_in),
        whole(seg_col),
        whole(seg_row),
    ]


@jax.custom_vjp
def attend(*operands):
    specs = attend_specs(*operands)
    pairs = operands[0].shape[1] // (PAIR * HEAD_SIZE)
    return run_kernel(
        attend_forward_kernel, operands, specs, [operands[0]], [specs[0]], pairs, 10**10
    )[0]


def attend_back(operands, cotangent):
    specs = attend_specs(*operands)
    pairs = operands[0].shape[1] // (PAIR * HEAD_SIZE)
    grads = run_kernel(
        attend_backward_kernel,
        operands + (cotangent,),
        specs + [specs[0]],
        operands[:3],
        specs[:3],
        pairs,
        3 * 10**10,
    )
    return tuple(grads) + (jnp.zeros_like(operands[3]), jnp.zeros_like(operands[4]))


attend.defvjp(lambda *operands: (attend(*operands), operands), attend_back)


def rotate(values):
    length, width = values.shape
    half = HEAD_SIZE // 2
    lane = jnp.arange(width, dtype=jnp.int32)
    position = jnp.arange(length, dtype=jnp.float32)
    frequency = THETA ** (-2.0 * jnp.arange(half, dtype=jnp.float32) / HEAD_SIZE)
    angles = position[:, None] * jnp.tile(frequency, width // half)[None, :]
    first = (lane % HEAD_SIZE < half)[None, :]
    later = jnp.concatenate([values[:, half:], values[:, :half]], 1)
    sooner = jnp.concatenate([values[:, -half:], values[:, :-half]], 1)
    return values * jnp.cos(angles) + jnp.where(first, -later, sooner) * jnp.sin(angles)


def mixer(
    inner_gate,
    state_in,
    step_raw,
    query,
    keyval,
    conv_inner,
    conv_state,
    step_bias,
    decay_log,
    skip_gain,
    segment_ids,
):
    inner_width = inner_gate.shape[1] // 2
    gate_in = inner_gate[:, :inner_width]
    inner = jax.nn.silu(causal_conv(inner_gate[:, inner_width:], conv_inner, segment_ids))
    maps = jax.nn.silu(causal_conv(state_in, conv_state, segment_ids))
    state_width = maps.shape[1] // 2
    step_size = jax.nn.softplus(step_raw + step_bias[None, :])
    decay_rate = -jnp.exp(decay_log)
    segment_float = segment_ids.astype(jnp.float32)
    seg_col, seg_row = segment_float[:, None], segment_float[None, :]
    columns, rows = scan_columns(step_size, decay_rate, segment_ids)
    scanned = pair_scan(
        inner, maps[:, :state_width], maps[:, state_width:], columns, rows, seg_col, seg_row
    )
    scanned = scanned + jnp.repeat(skip_gain, HEAD_SIZE)[None, :] * inner
    ssm_part = scanned * jax.nn.silu(gate_in)
    kv_width = keyval.shape[1] // 2
    attended = []
    key_heads = kv_width // HEAD_SIZE
    group = query.shape[1] // key_heads
    for head in range(key_heads):
        lanes = slice(HEAD_SIZE * head, HEAD_SIZE * (head + 1))
        attended.append(
            attend(
                rotate(query[:, group * head : group * (head + 1)] * HEAD_SIZE ** (-0.5)),
                rotate(keyval[:, :kv_width][:, lanes]),
                keyval[:, kv_width:][:, lanes],
                seg_col,
                seg_row,
            )
        )
    return jnp.concatenate([ssm_part] + attended, 1)


def rms_norm(values, gain):
    return values * lax.rsqrt(jnp.mean(values * values, axis=-1, keepdims=True) + EPS) * gain


def norm_back(values, gain, grad_normed):
    _, pullback = jax.vjp(rms_norm, values, gain)
    return pullback(grad_normed)


def matmul(left, right):
    return jnp.dot(left, right, preferred_element_type=jnp.float32)


def transposed_left(left, right):
    return lax.dot_general(
        left, right, (((0,), (0,)), ((), ())), preferred_element_type=jnp.float32
    )


def transposed_right(left, right):
    return lax.dot_general(
        left, right, (((1,), (1,)), ((), ())), preferred_element_type=jnp.float32
    )


SHARDS = ("dp", "row")


def pair_total(partial_value):
    own = partial_value.astype(jnp.bfloat16)
    other = lax.ppermute(own, "col", [(0, 1), (1, 0)])
    return own.astype(jnp.float32) + other.astype(jnp.float32)


def split_columns(array, widths):
    parts, start = [], 0
    for width in widths:
        parts.append(array[:, start : start + width])
        start += width
    return parts


def padded(parts):
    filled = sum(part.shape[1] for part in parts)
    gap = -filled % LANES
    return jnp.concatenate(
        list(parts) + [jnp.zeros((parts[0].shape[0], gap), parts[0].dtype)], 1
    )


def local(
    hidden_in,
    segments,
    mixer_gain,
    ssm_inner,
    state_proj,
    step_proj,
    query_proj,
    key_value_projection,
    conv_inner,
    conv_state,
    step_bias,
    decay_log,
    skip_gain,
    ssm_out,
    attn_out,
    ffn_gain,
    gate_up,
    down_proj,
    output_cotangent,
):
    share = ssm_inner.shape[0]
    in_parts = (
        ssm_inner.reshape(share, -1),
        state_proj,
        query_proj,
        key_value_projection.reshape(share, -1),
        step_proj,
        mixer_gain[:, None],
        ffn_gain[:, None],
    )
    in_widths = [part.shape[1] for part in in_parts]
    in_weight = lax.all_gather(padded(in_parts), SHARDS, axis=0, tiled=True)
    later_parts = (gate_up.reshape(share, -1), ssm_out.T, attn_out.T, down_proj.T)
    later_widths = [part.shape[1] for part in later_parts]
    later_weight = lax.all_gather(jnp.concatenate(later_parts, 1), SHARDS, axis=0, tiled=True)
    gain_mixer, gain_ffn = split_columns(in_weight, in_widths)[5:]
    gain_mixer, gain_ffn = gain_mixer[:, 0], gain_ffn[:, 0]
    gate_weight, ssm_weight, attn_weight, down_weight = split_columns(later_weight, later_widths)
    ssm_width = ssm_weight.shape[1]
    mixed_weight = later_weight[:, later_widths[0] : sum(later_widths[:3])]
    row_count = hidden_in.shape[0]
    model_width = hidden_in.shape[1]
    seq_count = row_count // SEQ_LEN
    segment_rows = segments.reshape(seq_count, SEQ_LEN)
    hidden = hidden_in.astype(jnp.float32)
    normed = rms_norm(hidden, gain_mixer.astype(jnp.float32)).astype(jnp.bfloat16)
    projected = matmul(normed, in_weight)
    inner_gate, state_in, query_in, keyval_in, step_raw = split_columns(projected, in_widths)[:5]

    def local_mixer(
        inner_part,
        state_part,
        step_part,
        query_part,
        keyval_part,
        inner_kernel,
        state_kernel,
        bias_part,
        decay_part,
        skip_part,
    ):

        def single(leading_input, second_in, third_in, fourth_in, fifth_in, sequence_ids):
            return mixer(
                leading_input,
                second_in,
                third_in,
                fourth_in,
                fifth_in,
                inner_kernel,
                state_kernel,
                bias_part,
                decay_part,
                skip_part,
                sequence_ids,
            )

        rows = []
        for index in range(seq_count):
            span = slice(index * SEQ_LEN, (index + 1) * SEQ_LEN)
            rows.append(
                single(
                    inner_part[span],
                    state_part[span],
                    step_part[span],
                    query_part[span],
                    keyval_part[span],
                    segment_rows[index],
                )
            )
        return jnp.concatenate(rows, 0)

    mixed_float, mixer_pull = jax.vjp(
        local_mixer,
        inner_gate,
        state_in,
        step_raw,
        query_in,
        keyval_in,
        conv_inner,
        conv_state,
        step_bias,
        decay_log,
        skip_gain,
    )
    mixed_out = mixed_float.astype(jnp.bfloat16)
    mixer_delta = pair_total(transposed_right(mixed_out, mixed_weight))
    middle = hidden + mixer_delta
    normed_ffn = rms_norm(middle, gain_ffn.astype(jnp.float32)).astype(jnp.bfloat16)
    gate_values = matmul(normed_ffn, gate_weight)
    half_width = gate_values.shape[1] // 2
    gate_part = gate_values[:, :half_width]
    up_part = gate_values[:, half_width:]
    hidden_ffn = (jax.nn.silu(gate_part) * up_part).astype(jnp.bfloat16)
    result = middle + pair_total(transposed_right(hidden_ffn, down_weight))
    hidden_out = result.astype(jnp.bfloat16)
    grad_down = transposed_left(output_cotangent, hidden_ffn)
    grad_hidden_ffn = (
        matmul(output_cotangent, down_weight).astype(jnp.bfloat16).astype(jnp.float32)
    )
    sigmoid_gate = jax.nn.sigmoid(gate_part)
    grad_gate = grad_hidden_ffn * up_part * sigmoid_gate * (1.0 + gate_part * (1.0 - sigmoid_gate))
    grad_up = grad_hidden_ffn * gate_part * sigmoid_gate
    grad_gate_values = jnp.concatenate([grad_gate, grad_up], 1).astype(jnp.bfloat16)
    grad_gate_weight = transposed_left(normed_ffn, grad_gate_values)
    grad_normed_ffn = pair_total(transposed_right(grad_gate_values, gate_weight))
    back_middle, grad_gain_ffn = norm_back(middle, gain_ffn.astype(jnp.float32), grad_normed_ffn)
    grad_middle = output_cotangent.astype(jnp.float32) + back_middle
    grad_delta = grad_middle.astype(jnp.bfloat16)
    grad_mixed_weight = transposed_left(grad_delta, mixed_out)
    later_grads = lax.psum_scatter(
        jnp.concatenate([grad_gate_weight, grad_mixed_weight, grad_down], 1).astype(jnp.bfloat16),
        SHARDS,
        scatter_dimension=0,
        tiled=True,
    ).astype(jnp.float32)
    grad_gate_up, grad_ssm_out, grad_attn_out, grad_down_proj = split_columns(
        later_grads, later_widths
    )
    grad_mixed = matmul(grad_delta, mixed_weight)
    grad_mixed = grad_mixed.astype(jnp.bfloat16).astype(jnp.float32)
    (
        grad_inner_gate,
        grad_state_in,
        raw_step_gradient,
        grad_query_in,
        grad_keyval_in,
        grad_conv_inner,
        conv_state_gradient,
        grad_step_bias,
        grad_decay_log,
        grad_skip_gain,
    ) = mixer_pull(grad_mixed)
    half_state = (0.5 * pair_total(grad_state_in)).astype(jnp.bfloat16)
    conv_state_gradient = conv_state_gradient + lax.ppermute(
        conv_state_gradient, "col", [(0, 1), (1, 0)]
    )
    small = (
        grad_conv_inner,
        conv_state_gradient,
        grad_step_bias,
        grad_decay_log,
        grad_skip_gain,
    )
    packed = lax.psum(jnp.concatenate([part.reshape(-1) for part in small]), SHARDS)
    unpacked, start = [], 0
    for part in small:
        unpacked.append(packed[start : start + part.size].reshape(part.shape))
        start += part.size
    grad_conv_inner, conv_state_gradient, grad_step_bias, grad_decay_log, grad_skip_gain = unpacked
    rounded = padded(
        [
            grad_inner_gate.astype(jnp.bfloat16),
            half_state,
            grad_query_in.astype(jnp.bfloat16),
            grad_keyval_in.astype(jnp.bfloat16),
            raw_step_gradient.astype(jnp.bfloat16),
            jnp.zeros((row_count, 2), jnp.bfloat16),
        ]
    )
    grad_normed = pair_total(transposed_right(rounded, in_weight))
    back_hidden, grad_gain_mixer = norm_back(hidden, gain_mixer.astype(jnp.float32), grad_normed)
    input_grad = grad_middle + back_hidden
    weight_grads = split_columns(transposed_left(normed, rounded), in_widths)[:5]
    weight_grads[1] = 2.0 * weight_grads[1]
    in_grads = lax.psum_scatter(
        padded(
            [
                part.astype(jnp.bfloat16)
                for part in weight_grads + [grad_gain_mixer[:, None], grad_gain_ffn[:, None]]
            ]
        ),
        SHARDS,
        scatter_dimension=0,
        tiled=True,
    ).astype(jnp.float32)
    (
        grad_ssm_inner,
        grad_state_proj,
        grad_query_proj,
        grad_keyval_proj,
        grad_step_proj,
        grad_mixer_gain,
        grad_ffn_gain,
    ) = split_columns(in_grads, in_widths)
    grad_ssm_inner = grad_ssm_inner.reshape(ssm_inner.shape)
    grad_keyval_proj = grad_keyval_proj.reshape(key_value_projection.shape)
    grad_gate_up = grad_gate_up.reshape(gate_up.shape)
    grad_mixer_gain, grad_ffn_gain = grad_mixer_gain[:, 0], grad_ffn_gain[:, 0]
    grad_ssm_out, grad_attn_out, grad_down_proj = (
        grad_ssm_out.T,
        grad_attn_out.T,
        grad_down_proj.T,
    )
    return (
        hidden_out,
        input_grad,
        grad_mixer_gain,
        grad_ssm_inner,
        grad_state_proj,
        grad_step_proj,
        grad_query_proj,
        grad_keyval_proj,
        grad_conv_inner,
        conv_state_gradient,
        grad_step_bias,
        grad_decay_log,
        grad_skip_gain,
        grad_ssm_out,
        grad_attn_out,
        grad_ffn_gain,
        grad_gate_up,
        grad_down_proj,
    )


def solution(mesh):
    placed = (
        P(("dp", "row"), None),
        P(("dp", "row")),
        P(("dp", "row")),
        P(("dp", "row"), None, "col"),
        P(("dp", "row"), None),
        P(("dp", "row"), "col"),
        P(("dp", "row"), "col"),
        P(("dp", "row"), None, "col"),
        P(None, "col"),
        P(),
        P("col"),
        P("col"),
        P("col"),
        P("col", ("dp", "row")),
        P("col", ("dp", "row")),
        P(("dp", "row")),
        P(("dp", "row"), None, "col"),
        P("col", ("dp", "row")),
        P(("dp", "row"), None),
    )
    return jax.shard_map(
        local,
        mesh=mesh,
        in_specs=placed,
        out_specs=(
            P(("dp", "row"), None),
            P(("dp", "row"), None),
            P(("dp", "row")),
            P(("dp", "row"), None, "col"),
            P(("dp", "row"), None),
            P(("dp", "row"), "col"),
            P(("dp", "row"), "col"),
            P(("dp", "row"), None, "col"),
            P(None, "col"),
            P(),
            P("col"),
            P("col"),
            P("col"),
            P("col", ("dp", "row")),
            P("col", ("dp", "row")),
            P(("dp", "row")),
            P(("dp", "row"), None, "col"),
            P("col", ("dp", "row")),
        ),
        check_vma=False,
    )
```

time: 2420 us -> 795 us (0.33)
  waiting for transfers between devices: 933 us -> 292 us
  matrix products: 408 us -> 71.6 us
  local copies, waits for them, and re-layouts: 437 us -> 113 us
  blocking collectives: 332 us -> 74.3 us
  other arithmetic: 228 us -> 124 us
  Pallas kernels: 0 us -> 90.7 us
  loops' own time: 44.3 us -> 0 us
    reduce_scatter x7 -> x2, waiting for transfers between devices: 559 us -> 194 us  [the longest x1 171 us: local(): lax.psum_scatter(jnp.concatenate([grad_gate_weight, grad_mixed_weight, gr...]
    dot_general x62 -> x2, matrix products: 290 us -> 1.92 us  [scan_columns(): running = jnp.einsum('ts,bsh->bth', lower, decay_blocks, precision=HIGH)]
    unnamed x19 -> x4, waiting for transfers between devices: 261 us -> 0.07 us
    dynamic_update_slice x72 -> x0, local copies, waits for them, and re-layouts: 224 us -> none  [state_scan(): lax.scan(advance, initial, (inner_blocks, input_blocks, output_blocks, st...]
    all_gather x5 -> x0, blocking collectives: 206 us -> none  [the longest x1 44.2 us: local(): lax.all_gather(key_value_projection, ('dp', 'row'), axis=0, tiled=True)]
    unnamed x2 -> x0, blocking collectives: 123 us -> none
    pallas_call x0 -> x4, Pallas kernels: none -> 90.7 us  [the longest x1 49.1 us: mixer(): pair_scan(inner, maps[:, :state_width], maps[:, state_width:], columns, r...]
    psum x1, blocking collectives: 2.76 us -> 74.3 us  [local(): lax.psum(jnp.concatenate([part.reshape(-1) for part in small]), SHARDS)]
  transfers between devices with their start and end apart: 17 -> 10, of which waited for: 12 -> 5; matrix products, arithmetic and copies ran while one was open for 31% -> 20% of each run, Pallas kernels for 0% -> 3%
where the time goes in v1:
time: 795 us; the launch traced here: 782 us
  waiting for transfers between devices  292 us (37%)
  other arithmetic  124 us (16%)
  local copies, waits for them, and re-layouts  113 us (14%)
  Pallas kernels  90.7 us (11%)
  blocking collectives  74.3 us (9%)
  matrix products  71.6 us (9%)
  between operations  15.9 us (2%)
    reduce_scatter x1, waiting for transfers between devices, local(): lax.psum_scatter(jnp.concatenate([grad_gate_weight, grad_mixed_weight, gr...  171 us
    psum x1, blocking collectives, local(): lax.psum(jnp.concatenate([part.reshape(-1) for part in small]), SHARDS)  74.3 us
    all_gather x1, waiting for transfers between devices, local(): in_weight = lax.all_gather(padded(in_parts), SHARDS, axis=0, tiled=True)  71.9 us
    pallas_call x1, Pallas kernels, mixer(): pair_scan(inner, maps[:, :state_width], maps[:, state_width:], columns, r...  49.1 us
    dot_general x4, matrix products, matmul(): return jnp.dot(left, right, preferred_element_type=jnp.float32)  26.8 us
    pallas_call x2, Pallas kernels, run_kernel(): pl.pallas_call(body, grid=(grid,), in_specs=in_specs, out_specs=out_specs...  25.2 us
    unnamed x266, local copies, waits for them, and re-layouts  24.9 us
    reduce_scatter x1, waiting for transfers between devices, local(): lax.psum_scatter(padded([part.astype(jnp.bfloat16) for part in weight_gra...  23.3 us
  transfers between devices with their start and end apart: 10, of which 5 were waited for; matrix products, arithmetic and copies ran while one was open for 20% of the time, Pallas kernels for 3%

profile of v1, /device:TPU:0, one launch (start us, length us, event | category | flops | bytes accessed | tf_op | source)
XLA Modules:
  0.0 782.4 jit_solution(3398478872507893079)
XLA Ops:
  24.4 71.9 %all-gather.3.cloned.1.call-done = bf16[1024,2304]{1,0:T(8,128)(2,1)} async-done(((bf16[64,2304]{1,0:T(8,128)(2,1)}), bf16[1024,2304]{1,0:T(8,128)(2,1)}) %all-gather.3.cloned.1.call-update) | async-done | bytes 4718608 | tf_op jit(solution)/shard_map/all_gather | solution.py:489
  98.4 10.1 %fusion.47 = f32[1024,2304]{1,0:T(8,128)} fusion(bf16[1024,2304]{1,0:T(8,128)(2,1)} %all-gather.3.cloned.1.call-done, bf16[1024,1024]{0,1:T(8,128)(2,1)S(1)} %copy.235, f32[1024]{0:T(1024)S(1)} %get-tuple-element.147, f32[1024]{0:T(1024)S(1)} %fusion.77), kind=kOutput, calls=%fused_computation.117 | convolution fusion | flops 4836032512 | bytes 16261120 | tf_op jit(solution)/shard_map/dot_general | solution.py:417
  143.7 8.0 %fusion.43 = (f32[1024,256]{1,0:T(8,128)S(1)}, f32[1024,256]{1,0:T(8,128)}, f32[1024,256]{1,0:T(8,128)S(1)}) fusion(f32[1024]{0:T(1024)S(1)} %get-tuple-element.240, f32[256]{0:T(256)S(1)} %bitcast.193, f32[1021,256]{1,0:T(8,128)S(1)} %copy-done.38, f32[1024]{0:T(1024)S(1)} %get-tuple-element.241, f32[256]{0:T(256)S(1)} %bitcast.197, ...), kind=kLoop, calls=%fused_computation.112 | loop fusion | flops 6029312 | bytes 10497280 | tf_op jit(solution)/shard_map/jvp(jit(silu))/mul | solution.py:377
  151.7 7.6 jvp__.3
  162.4 6.1 fusion.24
  168.4 17.6 %jvp__.2 = f32[1024,768]{1,0:T(8,128)S(1)} custom-call(f32[1024,768]{1,0:T(8,128)} %get-tuple-element.180.inner, f32[1024,128]{1,0:T(8,128)S(1)} %get-tuple-element.205.input_map, f32[1024,128]{1,0:T(8,128)S(1)} %get-tuple-element.204.output_map, f32[6,1024,8]{2,1,0:T(8,128)} %copy.252.columns, f32[6,4,1024]{2,1,0:T(4,128)S(1)} %reshape.398.rows, ...), custom_call_target="tpu_custom_call" | custom-call | flops 10000000000 | bytes 67108864 | tf_op jit(solution)/shard_map/jvp()/pallas_call | solution.py:197
  186.0 4.2 multiply_convert_fusion.2
  190.2 21.0 %all-gather.5.cloned.1.call-done = bf16[1024,4096]{1,0:T(8,128)(2,1)} async-done(((bf16[64,4096]{1,0:T(8,128)(2,1)}), bf16[1024,4096]{1,0:T(8,128)(2,1)}) %all-gather.5.cloned.1.call-update) | async-done | bytes 8388624 | tf_op jit(solution)/shard_map/all_gather | solution.py:492
  211.2 4.7 convolution_convert_fusion.5
  216.0 4.1 collective-permute-done
  223.7 6.9 fusion.17
  230.6 4.2 fusion.10
  234.8 5.8 fusion.25
  248.7 5.6 multiply_reduce_fusion
  254.4 7.5 fusion.4
  261.9 5.6 convert_convert_fusion
  267.6 6.6 multiply_reduce_fusion.3
  274.4 16.5 %transpose_jvp___.3 = (f32[1024,256]{1,0:T(8,128)S(1)}, f32[1024,64]{1,0:T(8,128)S(1)}, f32[1024,64]{1,0:T(8,128)S(1)}) custom-call(f32[1024,256]{1,0:T(8,128)S(1)} %copy-done.1, f32[1024,64]{1,0:T(8,128)S(1)} %copy-done.8, f32[1024,64]{1,0:T(8,128)S(1)} %copy-done.6, f32[1024,1]{1,0:T(8,128)S(1)} %copy-done.4, f32[1,1024]{1,0:T(1,128)S(1)} %bitcast.164, ...), custom_call_target="tpu_custom_call" | custom-call | flops 30000001024 | bytes 67108864 | tf_op jit(solution)/shard_map/transpose(jvp())/pallas_call | solution.py:396
  290.9 4.9 fusion.44
  297.9 49.1 %transpose_jvp___.2 = (f32[1024,768]{1,0:T(8,128)S(1)}, f32[1024,128]{1,0:T(8,128)S(1)}, f32[1024,128]{1,0:T(8,128)S(1)}, f32[6,1024,8]{2,1,0:T(8,128)}, f32[6,4,1024]{2,1,0:T(4,128)S(1)}) custom-call(f32[1024,768]{1,0:T(8,128)} %get-tuple-element.180.inner, f32[1024,128]{1,0:T(8,128)S(1)} %copy-done.12, f32[1024,128]{1,0:T(8,128)S(1)} %copy-done.10, ...), custom_call_target="tpu_custom_call" | custom-call | flops 30000001024 | bytes 67108864 | tf_op jit(solution)/shard_map/transpose(jvp())/pallas_call | solution.py:384
  410.2 5.8 multiply_convert_fusion.3
  419.3 7.0 concatenate.93
  426.3 8.7 %convolution_convert_fusion.3 = bf16[1024,1024]{0,1:T(8,128)(2,1)S(1)} fusion(bf16[1024,2304]{1,0:T(8,128)(2,1)} %concatenate.93, bf16[1024,2304]{1,0:T(8,128)(2,1)} %all-gather.3.cloned.1.call-done), kind=kOutput, calls=%fused_computation.70 | convolution fusion | flops 4832886784 | bytes 11534336 | tf_op jit(solution)/shard_map/dot_general | solution.py:427
  436.4 5.1 fusion.106
  447.2 7.6 concatenate.94
  454.9 4.8 convert_bitcast_fusion
  459.8 7.7 convolution_convert_fusion
  479.2 74.3 %psum.7 = f32[4132]{0:T(1024)S(1)} all-reduce(f32[4132]{0:T(1024)S(1)} %concatenate.95), channel_id=1, replica_groups=mesh['dp'=4,'row'=4,'col'=2] {'dp','row'}, use_global_device_ids=true, to_apply=%region_21.22 | all-reduce | flops 4132 | bytes 33056 | tf_op jit(solution)/shard_map/psum | solution.py:622
  555.3 6.8 fusion.5
  562.2 5.4 copy.278
  567.6 23.3 %reduce-scatter.3.cloned.1.call-done = bf16[64,2304]{1,0:T(8,128)(2,1)} async-done(((bf16[1024,2304]{1,0:T(8,128)(2,1)}), bf16[64,2304]{1,0:T(8,128)(2,1)}) %reduce-scatter.3.cloned.1.call-update) | async-done | bytes 294928 | tf_op jit(solution)/shard_map/reduce_scatter | solution.py:643
  598.9 171.1 %reduce-scatter.5.cloned.1.call-done = bf16[64,4096]{1,0:T(8,128)(2,1)} async-done(((bf16[1024,4096]{1,0:T(8,128)(2,1)}), bf16[64,4096]{1,0:T(8,128)(2,1)}) %reduce-scatter.5.cloned.1.call-update) | async-done | bytes 524304 | tf_op jit(solution)/shard_map/reduce_scatter | solution.py:588
  (448 shorter events, 170.8 us)
Async XLA Ops:
  7.2 89.1 %all-gather.3.cloned.1.call-start = ((), (), s32[]{:S(2)}) async-start(), calls=%async_computation.2 | async-start | bytes 5013504 | tf_op jit(solution)/shard_map/all_gather | solution.py:489
  13.0 198.2 %all-gather.5.cloned.1.call-start = ((), (), s32[]{:S(2)}) async-start(), calls=%async_computation.3 | async-start | bytes 8912896 | tf_op jit(solution)/shard_map/all_gather | solution.py:492
  15.9 575.0 %reduce-scatter.3.cloned.1.call-start = ((), (), s32[]{:S(2)}) async-start(), calls=%async_computation.4 | async-start | bytes 5013504 | tf_op jit(solution)/shard_map/reduce_scatter | solution.py:643
  18.9 89.5 %copy-start.13 = (bf16[1024,1024]{0,1:T(8,128)(2,1)}, bf16[1024,1024]{0,1:T(8,128)(2,1)S(1)}, u32[]{:S(2)}) copy-start(bf16[1024,1024]{0,1:T(8,128)(2,1)S(1)} %copy.235) | copy-start | bytes 6291460
  20.6 108.8 %copy-start.105 = (f32[4]{0:T(128)}, f32[4]{0:T(128)S(1)}, u32[]{:S(2)}) copy-start(f32[4]{0:T(128)S(1)} %get-tuple-element.174) | copy-start | bytes 52
  20.8 109.3 %copy-start.55 = (f32[4,256]{0,1:T(8,128)}, f32[4,256]{0,1:T(8,128)S(1)}, u32[]{:S(2)}) copy-start(f32[4,256]{0,1:T(8,128)S(1)} %copy.245) | copy-start | bytes 12292
  20.9 109.1 %copy-start.60 = (f32[4,256]{0,1:T(8,128)}, f32[4,256]{0,1:T(8,128)S(1)}, u32[]{:S(2)}) copy-start(f32[4,256]{0,1:T(8,128)S(1)} %copy.243) | copy-start | bytes 12292
  21.1 269.8 %copy-start.85 = (f32[256]{0:T(256)}, f32[256]{0:T(256)S(1)}, u32[]{:S(2)}) copy-start(f32[256]{0:T(256)S(1)} %mul.734) | copy-start | bytes 3076
  21.3 130.4 %copy-start.2 = (f32[1024,1]{1,0:T(8,128)}, f32[1024,1]{1,0:T(8,128)S(1)}, u32[]{:S(2)}) copy-start(f32[1024,1]{1,0:T(8,128)S(1)} %copy.253.seg_col) | copy-start | bytes 12292
  23.1 137.2 %copy-start.75 = (f32[768]{0:T(1024)}, f32[768]{0:T(1024)S(1)}, u32[]{:S(2)}) copy-start(f32[768]{0:T(1024)S(1)} %get-tuple-element.152) | copy-start | bytes 9220
  23.1 137.2 %copy-start.77 = (f32[768]{0:T(1024)}, f32[768]{0:T(1024)S(1)}, u32[]{:S(2)}) copy-start(f32[768]{0:T(1024)S(1)} %get-tuple-element.151) | copy-start | bytes 9220
  23.2 137.2 %copy-start.79 = (f32[768]{0:T(1024)}, f32[768]{0:T(1024)S(1)}, u32[]{:S(2)}) copy-start(f32[768]{0:T(1024)S(1)} %get-tuple-element.153) | copy-start | bytes 9220
  23.2 137.2 %copy-start.81 = (f32[768]{0:T(1024)}, f32[768]{0:T(1024)S(1)}, u32[]{:S(2)}) copy-start(f32[768]{0:T(1024)S(1)} %get-tuple-element.150) | copy-start | bytes 9220
  23.2 85.2 %copy-start.112 = (f32[12]{0:T(128)}, f32[12]{0:T(128)S(1)}, u32[]{:S(2)}) copy-start(f32[12]{0:T(128)S(1)} %exponential_negate_fusion) | copy-start | bytes 148
  23.7 74.1 %copy-start.73 = (f32[1024]{0:T(1024)}, f32[1024]{0:T(1024)S(1)}, u32[]{:S(2)}) copy-start(f32[1024]{0:T(1024)S(1)} %fusion.77) | copy-start | bytes 12292
  24.3 119.3 %copy-start.92 = (f32[1,256]{1,0:T(1,128)}, f32[1,256]{1,0:T(1,128)S(1)}, u32[]{:S(2)}) copy-start(f32[1,256]{1,0:T(1,128)S(1)} %get-tuple-element.237) | copy-start | bytes 3076
  97.8 156.6 %copy-start.67 = (f32[1024]{0:T(1024)}, f32[1024]{0:T(1024)S(1)}, u32[]{:S(2)}) copy-start(f32[1024]{0:T(1024)S(1)} %get-tuple-element.146) | copy-start | bytes 12292
  109.8 21.9 %copy-start.27 = (f32[1024,12]{1,0:T(8,128)}, f32[1024,12]{1,0:T(8,128)S(1)}, u32[]{:S(2)}) copy-start(f32[1024,12]{1,0:T(8,128)S(1)} %get-tuple-element.177) | copy-start | bytes 147460
  111.0 19.0 %copy-start.42 = (f32[4,12,256]{1,0,2:T(4,128)}, f32[4,12,256]{1,0,2:T(4,128)S(1)}, u32[]{:S(2)}) copy-start(f32[4,12,256]{1,0,2:T(4,128)S(1)} %copy.240) | copy-start | bytes 147460
  113.1 30.6 %copy-start.34 = (f32[1023,256]{1,0:T(8,128)}, f32[1023,256]{1,0:T(8,128)S(1)}, u32[]{:S(2)}) copy-start(f32[1023,256]{1,0:T(8,128)S(1)} %slice.300) | copy-start | bytes 3142660
  215.9 4.2 collective-permute-start
  223.7 30.7 %copy-start.69 = (f32[1024]{0:T(1024)}, f32[1024]{0:T(1024)S(1)}, u32[]{:S(2)}) copy-start(f32[1024]{0:T(1024)S(1)} %fusion.78) | copy-start | bytes 12292
  240.6 8.1 %collective-permute-start.2 = (bf16[1024,1024]{0,1:T(8,128)(2,1)}, bf16[1024,1024]{0,1:T(8,128)(2,1)}, u32[]{:S(2)}, u32[]{:S(2)}) collective-permute-start(bf16[1024,1024]{0,1:T(8,128)(2,1)} %fusion.25), channel_id=1, source_target_pairs={{0,1},{1,0},{2,3},{3,2},{4,5},{5,4},{6,7},{7,6},{8,9},{9,8},{10,11... | collective-permute-start | bytes 6291464 | tf_op jit(solution)/shard_map/ppermute | solution.py:437
  244.4 9.9 %collective-permute-start.1 = (bf16[1024,1024]{0,1:T(8,128)(2,1)}, bf16[1024,1024]{0,1:T(8,128)(2,1)}, u32[]{:S(2)}, u32[]{:S(2)}) collective-permute-start(bf16[1024,1024]{0,1:T(8,128)(2,1)} %convolution_convert_fusion.4), channel_id=1, source_target_pairs={{0,1},{1,0},{2,3},{3,2},{4,5},{5,4},{6,7},{7,6},{8,9},{9,8},{10,11... | collective-permute-start | bytes 6291464 | tf_op jit(solution)/shard_map/ppermute | solution.py:437
  297.9 49.1 %copy-start.39 = (f32[1021,256]{1,0:T(8,128)S(1)}, f32[1021,256]{1,0:T(8,128)}, u32[]{:S(2)}) copy-start(f32[1021,256]{1,0:T(8,128)} %slice.302) | copy-start | bytes 3136516
  366.4 18.0 %copy-start.56 = (f32[4,256]{0,1:T(8,128)S(1)}, f32[4,256]{0,1:T(8,128)}, u32[]{:S(2)}) copy-start(f32[4,256]{0,1:T(8,128)} %copy-done.55) | copy-start | bytes 12292
  371.2 18.2 %copy-start.61 = (f32[4,256]{0,1:T(8,128)S(1)}, f32[4,256]{0,1:T(8,128)}, u32[]{:S(2)}) copy-start(f32[4,256]{0,1:T(8,128)} %copy-done.60) | copy-start | bytes 12292
  401.0 15.3 %collective-permute-start.3 = (bf16[1024,256]{1,0:T(8,128)(2,1)}, bf16[1024,256]{1,0:T(8,128)(2,1)}, u32[]{:S(2)}, u32[]{:S(2)}) collective-permute-start(bf16[1024,256]{1,0:T(8,128)(2,1)} %get-tuple-element.201), channel_id=1, source_target_pairs={{0,1},{1,0},{2,3},{3,2},{4,5},{5,4},{6,7},{7,6},{8,9},{9,8},{10,11... | collective-permute-start | bytes 1572872 | tf_op jit(solution)/shard_map/ppermute | solution.py:437
  435.0 9.4 %collective-permute-start.4 = (bf16[1024,1024]{0,1:T(8,128)(2,1)S(1)}, bf16[1024,1024]{0,1:T(8,128)(2,1)S(1)}, u32[]{:S(2)}, u32[]{:S(2)}) collective-permute-start(bf16[1024,1024]{0,1:T(8,128)(2,1)S(1)} %convolution_convert_fusion.3), channel_id=1, source_target_pairs={{0,1},{1,0},{2,3},{3,2},{4,5},{5,4},{6,7},{7,6},{8,9},{9,8},{10,11... | collective-permute-start | bytes 6291464 | tf_op jit(solution)/shard_map/ppermute | solution.py:437
  454.9 315.1 %reduce-scatter.5.cloned.1.call-start = ((), (), s32[]{:S(2)}) async-start(), calls=%async_computation.5 | async-start | bytes 8912896 | tf_op jit(solution)/shard_map/reduce_scatter | solution.py:588
  473.8 81.5 %copy-start.66 = (f32[1024]{0:T(1024)S(1)}, f32[1024]{0:T(1024)}, u32[]{:S(2)}) copy-start(f32[1024]{0:T(1024)} %copy-done.65) | copy-start | bytes 12292
  474.4 4.7 collective-permute-start.5
  (104 other events, 569.5 us)
Sparse Core Ops, SparseCore 0:
  13.1 83.1 all-gather.2
  99.6 111.4 all-gather.4
  455.0 135.9 reduce-scatter.2
  593.2 176.7 reduce-scatter.4

commit v2 on v1

--- a/solution.py
+++ b/solution.py
@@ -436,6 +436,49 @@
     own = partial_value.astype(jnp.bfloat16)
     other = lax.ppermute(own, "col", [(0, 1), (1, 0)])
     return own.astype(jnp.float32) + other.astype(jnp.float32)
+
+
+def index_bits():
+    bits = []
+    for axis in ("row", "dp"):
+        size = lax.psum(1, axis)
+        bits += [(axis, 1 << power) for power in range(size.bit_length() - 1)]
+    return bits
+
+
+def partner_value(value, bit):
+    axis, step = bit
+    size = lax.psum(1, axis)
+    return lax.ppermute(value, axis, [(index, index ^ step) for index in range(size)])
+
+
+def all_sum(value):
+    for bit in index_bits():
+        value = value + partner_value(value, bit)
+    return value
+
+
+def scatter_sum(array):
+    bits = index_bits()
+    tiles = array.shape[1] // LANES
+    edges = [LANES * (tiles * part // 3) for part in range(4)]
+    results = []
+    for part in range(3):
+        left = bits[::-1]
+        held = array[:, edges[part] : edges[part + 1]]
+        held = held.reshape((2,) * len(bits) + (-1, held.shape[1]))
+        for bit in bits[part:] + bits[:part]:
+            at = left.index(bit)
+            left.pop(at)
+            mine = lax.axis_index(bit[0]) // bit[1] % 2
+            sent = lax.dynamic_index_in_dim(held, 1 - mine, at, keepdims=False)
+            kept = lax.dynamic_index_in_dim(held, mine, at, keepdims=False)
+            got = partner_value(sent, bit)
+            held = kept.astype(jnp.float32) + got.astype(jnp.float32)
+            if left:
+                held = held.astype(jnp.bfloat16)
+        results.append(held)
+    return jnp.concatenate(results, 1)
 
 
 def split_columns(array, widths):
@@ -585,12 +628,9 @@
     grad_middle = output_cotangent.astype(jnp.float32) + back_middle
     grad_delta = grad_middle.astype(jnp.bfloat16)
     grad_mixed_weight = transposed_left(grad_delta, mixed_out)
-    later_grads = lax.psum_scatter(
+    later_grads = scatter_sum(
         jnp.concatenate([grad_gate_weight, grad_mixed_weight, grad_down], 1).astype(jnp.bfloat16),
-        SHARDS,
-        scatter_dimension=0,
-        tiled=True,
-    ).astype(jnp.float32)
+    )
     grad_gate_up, grad_ssm_out, grad_attn_out, grad_down_proj = split_columns(
         later_grads, later_widths
     )
@@ -619,7 +659,7 @@
         grad_decay_log,
         grad_skip_gain,
     )
-    packed = lax.psum(jnp.concatenate([part.reshape(-1) for part in small]), SHARDS)
+    packed = all_sum(jnp.concatenate([part.reshape(-1) for part in small]))
     unpacked, start = [], 0
     for part in small:
         unpacked.append(packed[start : start + part.size].reshape(part.shape))
@@ -640,17 +680,14 @@
     input_grad = grad_middle + back_hidden
     weight_grads = split_columns(transposed_left(normed, rounded), in_widths)[:5]
     weight_grads[1] = 2.0 * weight_grads[1]
-    in_grads = lax.psum_scatter(
+    in_grads = scatter_sum(
         padded(
             [
                 part.astype(jnp.bfloat16)
                 for part in weight_grads + [grad_gain_mixer[:, None], grad_gain_ffn[:, None]]
             ]
         ),
-        SHARDS,
-        scatter_dimension=0,
-        tiled=True,
-    ).astype(jnp.float32)
+    )
     (
         grad_ssm_inner,
         grad_state_proj,

time: 795 us -> 719 us (0.904)
  blocking collectives: 74.3 us -> 0 us
  waiting for transfers between devices: 292 us -> 256 us
  starting transfers between devices: 1.74 us -> 29.4 us
    reduce_scatter x2 -> x0, waiting for transfers between devices: 194 us -> none  [the longest x1 171 us: local(): lax.psum_scatter(jnp.concatenate([grad_gate_weight, grad_mixed_weight, gr...]
    ppermute x0 -> x28, waiting for transfers between devices: none -> 149 us  [partner_value(): lax.ppermute(value, axis, [(index, index ^ step) for index in range(size)])]
    psum x1 -> x0, blocking collectives: 74.3 us -> none  [local(): lax.psum(jnp.concatenate([part.reshape(-1) for part in small]), SHARDS)]
    ppermute x0 -> x28, starting transfers between devices: none -> 28.6 us  [partner_value(): lax.ppermute(value, axis, [(index, index ^ step) for index in range(size)])]
    all_gather x1, waiting for transfers between devices: 21 us -> 32.6 us  [local(): lax.all_gather(jnp.concatenate(later_parts, 1), SHARDS, axis=0, tiled=True)]
    convert_element_type x2 -> x18, other arithmetic: 2.11 us -> 11.3 us  [scatter_sum(): held = held.astype(jnp.bfloat16)]
    dynamic_slice x0 -> x8, local copies, waits for them, and re-layouts: none -> 8.39 us  [the longest x4 4.66 us: scatter_sum(): kept = lax.dynamic_index_in_dim(held, mine, at, keepdims=False)]
    slice x6, local copies, waits for them, and re-layouts: 17.6 us -> 9.37 us  [causal_conv(): signal[:length - offset]]
  transfers between devices with their start and end apart: 10 -> 36, of which waited for: 5 -> 21; matrix products, arithmetic and copies ran while one was open for 20% -> 38% of each run, Pallas kernels for 3% -> 13%
where the time goes in v2:
time: 719 us; the launch traced here: 708 us
  waiting for transfers between devices  256 us (36%)
  other arithmetic  130 us (18%)
  local copies, waits for them, and re-layouts  106 us (15%)
  Pallas kernels  91.2 us (13%)
  matrix products  79.5 us (11%)
  starting transfers between devices  29.4 us (4%)
  between operations  16.3 us (2%)
    ppermute x28, waiting for transfers between devices, partner_value(): lax.ppermute(value, axis, [(index, index ^ step) for index in range(size)])  149 us
    all_gather x1, waiting for transfers between devices, local(): in_weight = lax.all_gather(padded(in_parts), SHARDS, axis=0, tiled=True)  70.2 us
    pallas_call x1, Pallas kernels, mixer(): pair_scan(inner, maps[:, :state_width], maps[:, state_width:], columns, r...  49.6 us
    all_gather x1, waiting for transfers between devices, local(): lax.all_gather(jnp.concatenate(later_parts, 1), SHARDS, axis=0, tiled=True)  32.6 us
    dot_general x4, matrix products, transposed_right(): lax.dot_general(left, right, (((1,), (1,)), ((), ())), preferred_element_...  29.2 us
    ppermute x28, starting transfers between devices, partner_value(): lax.ppermute(value, axis, [(index, index ^ step) for index in range(size)])  28.6 us
    unnamed x262, local copies, waits for them, and re-layouts  25 us
    pallas_call x2, Pallas kernels, run_kernel(): pl.pallas_call(body, grid=(grid,), in_specs=in_specs, out_specs=out_specs...  24.9 us
  transfers between devices with their start and end apart: 36, of which 21 were waited for; matrix products, arithmetic and copies ran while one was open for 38% of the time, Pallas kernels for 13%

profile of v2, /device:TPU:0, one launch (start us, length us, event | category | flops | bytes accessed | tf_op | source)
XLA Modules:
  0.0 708.4 jit_solution(605724470222159044)
XLA Ops:
  26.0 70.2 %all-gather.3.cloned.1.call-done = bf16[1024,2304]{1,0:T(8,128)(2,1)} async-done(((bf16[64,2304]{1,0:T(8,128)(2,1)}), bf16[1024,2304]{1,0:T(8,128)(2,1)}) %all-gather.3.cloned.1.call-update) | async-done | bytes 4718608 | tf_op jit(solution)/shard_map/all_gather | solution.py:532
  97.7 7.6 %fusion.62 = f32[1024,2304]{1,0:T(8,128)S(1)} fusion(bf16[1024,2304]{1,0:T(8,128)(2,1)} %all-gather.3.cloned.1.call-done, bf16[1024,1024]{0,1:T(8,128)(2,1)S(1)} %copy.295, f32[1024]{0:T(1024)S(1)} %get-tuple-element.147, f32[1024]{0:T(1024)S(1)} %fusion.96), kind=kOutput, calls=%fused_computation.161 | convolution fusion | flops 4836032512 | bytes 16261120 | tf_op jit(solution)/shard_map/dot_general | solution.py:417
  124.5 8.2 %fusion.52 = (f32[1024,256]{1,0:T(8,128)}, f32[1024,256]{1,0:T(8,128)}, f32[1024,256]{1,0:T(8,128)S(1)}) fusion(f32[1024]{0:T(1024)S(1)} %get-tuple-element.252, f32[256]{0:T(256)S(1)} %bitcast.345, f32[1021,256]{1,0:T(8,128)S(1)} %copy-done.39, f32[1024]{0:T(1024)S(1)} %get-tuple-element.253, f32[256]{0:T(256)S(1)} %bitcast.347, ...), kind=kLoop, calls=%fused_computation.137 | loop fusion | flops 6029312 | bytes 10497280 | tf_op jit(solution)/shard_map/jvp(jit(silu))/mul | solution.py:377
  132.7 7.3 %jvp__.3 = f32[1024,256]{1,0:T(8,128)S(1)} custom-call(f32[1024,256]{1,0:T(8,128)S(1)} %get-tuple-element.185.queries, f32[1024,64]{1,0:T(8,128)S(1)} %get-tuple-element.187.keys_in, f32[1024,64]{1,0:T(8,128)S(1)} %get-tuple-element.186.values_in, f32[1024,1]{1,0:T(8,128)S(1)} %copy.313.seg_col, f32[1,1024]{1,0:T(1,128)S(1)} %bitcast.303), custom_call_target="tpu_custom_call" | custom-call | flops 10000000000 | bytes 67108864 | tf_op jit(solution)/shard_map/jvp()/pallas_call | solution.py:197
  149.5 6.8 fusion.24
  156.4 17.6 %jvp__.2 = f32[1024,768]{1,0:T(8,128)S(1)} custom-call(f32[1024,768]{1,0:T(8,128)} %get-tuple-element.180.inner, f32[1024,128]{1,0:T(8,128)S(1)} %get-tuple-element.217.input_map, f32[1024,128]{1,0:T(8,128)S(1)} %get-tuple-element.216.output_map, f32[6,1024,8]{2,1,0:T(8,128)} %copy.312.columns, f32[6,4,1024]{2,1,0:T(4,128)S(1)} %reshape.477.rows, ...), custom_call_target="tpu_custom_call" | custom-call | flops 10000000000 | bytes 67108864 | tf_op jit(solution)/shard_map/jvp()/pallas_call | solution.py:197
  178.5 32.6 %all-gather.5.cloned.1.call-done = bf16[1024,4096]{1,0:T(8,128)(2,1)} async-done(((bf16[64,4096]{1,0:T(8,128)(2,1)}), bf16[1024,4096]{1,0:T(8,128)(2,1)}) %all-gather.5.cloned.1.call-update) | async-done | bytes 8388624 | tf_op jit(solution)/shard_map/all_gather | solution.py:535
  211.1 5.9 convolution_convert_fusion.5
  230.6 5.6 fusion.10
  236.2 7.5 %convolution_convert_fusion = bf16[1024,2048]{1,0:T(8,128)(2,1)S(1)} fusion(bf16[1024,1024]{1,0:T(8,128)(2,1)} %get-tuple-element.184, bf16[1024,1024]{1,0:T(8,128)(2,1)S(1)} %get-tuple-element.183, f32[1024,1024]{0,1:T(8,128)S(1)} %get-tuple-element.173, f32[1024]{0:T(1024)S(1)} %get-tuple-element.146, f32[1024]{0:T(1024)S(1)} %fusion.97), kind=kOutput, calls=%fused_computation.37 | convolution fusion | flops 4308598784 | bytes 12591104 | tf_op jit(solution)/shard_map/dot_general | solution.py:421
  248.6 9.4 %fusion.28 = bf16[1024,1024]{0,1:T(8,128)(2,1)} fusion(bf16[1024,4096]{1,0:T(8,128)(2,1)} %all-gather.5.cloned.1.call-done, bf16[1024,1024]{1,0:T(8,128)(2,1)} %get-tuple-element.184, bf16[1024,1024]{1,0:T(8,128)(2,1)} %copy-done.123), kind=kOutput, calls=%fused_computation.74 | convolution fusion | flops 4304404480 | bytes 10485760 | tf_op jit(solution)/shard_map/dot_general | solution.py:427
  258.0 20.5 %collective-permute-done.30 = bf16[2,2,2,64,1280]{4,3,0,1,2:T(8,128)(2,1)} collective-permute-done((bf16[2,2,2,64,1280]{4,3,0,1,2:T(8,128)(2,1)}, bf16[2,2,2,64,1280]{4,3,0,1,2:T(8,128)(2,1)}, u32[]{:S(2)}, u32[]{:S(2)}) %collective-permute-start.30) | collective-permute-done | bytes 1310752 | tf_op jit(solution)/shard_map/ppermute | solution.py:452
  283.5 5.3 convolution_convert_fusion.4
  292.8 6.1 convert_bitcast_fusion
  306.7 6.7 fusion.4
  313.4 5.6 convert_convert_fusion
  319.1 6.6 multiply_reduce_fusion.3
  333.5 49.6 %transpose_jvp___.2 = (f32[1024,768]{1,0:T(8,128)S(1)}, f32[1024,128]{1,0:T(8,128)S(1)}, f32[1024,128]{1,0:T(8,128)S(1)}, f32[6,1024,8]{2,1,0:T(8,128)}, f32[6,4,1024]{2,1,0:T(4,128)S(1)}) custom-call(f32[1024,768]{1,0:T(8,128)} %get-tuple-element.180.inner, f32[1024,128]{1,0:T(8,128)S(1)} %copy-done.14, f32[1024,128]{1,0:T(8,128)S(1)} %copy-done.12, ...), custom_call_target="tpu_custom_call" | custom-call | flops 30000001024 | bytes 67108864 | tf_op jit(solution)/shard_map/transpose(jvp())/pallas_call | solution.py:384
  402.5 16.6 %transpose_jvp___.3 = (f32[1024,256]{1,0:T(8,128)S(1)}, f32[1024,64]{1,0:T(8,128)S(1)}, f32[1024,64]{1,0:T(8,128)S(1)}) custom-call(f32[1024,256]{1,0:T(8,128)S(1)} %copy-done.1, f32[1024,64]{1,0:T(8,128)S(1)} %copy-done.10, f32[1024,64]{1,0:T(8,128)S(1)} %copy-done.8, f32[1024,1]{1,0:T(8,128)S(1)} %copy-done.4, f32[1,1024]{1,0:T(1,128)S(1)} %bitcast.306, ...), custom_call_target="tpu_custom_call" | custom-call | flops 30000001024 | bytes 67108864 | tf_op jit(solution)/shard_map/transpose(jvp())/pallas_call | solution.py:396
  445.4 6.8 multiply_reduce_fusion.4
  474.0 22.0 %collective-permute-done.19 = f32[4132]{0:T(1024)S(1)} collective-permute-done((f32[4132]{0:T(1024)S(1)}, f32[4132]{0:T(1024)S(1)}, u32[]{:S(2)}, u32[]{:S(2)}) %collective-permute-start.19) | collective-permute-done | bytes 16560 | tf_op jit(solution)/shard_map/ppermute | solution.py:452
  517.1 7.9 %concatenate.118 = bf16[1024,2304]{1,0:T(8,128)(2,1)} concatenate(bf16[1024,1536]{1,0:T(8,128)(2,1)} %add_convert_fusion, bf16[1024,256]{1,0:T(8,128)(2,1)S(1)} %multiply_convert_fusion.4, bf16[1024,256]{1,0:T(8,128)(2,1)S(1)} %multiply_convert_fusion.3, bf16[1024,128]{1,0:T(8,128)(2,1)} %add_convert_fusion.3, bf16[1024,12]{1,0:T(8,128)(2,1)S(1)} %get-tuple-element.157, ...), dimensions={1} | concatenate | bytes 9437184 | tf_op jit(solution)/shard_map/concatenate | solution.py:495
  525.1 7.5 %fusion.126 = (bf16[1024,2304]{1,0:T(8,128)(2,1)S(1)}, f32[1024,2304]{1,0:T(8,128)S(1)}) fusion(bf16[1024,2304]{1,0:T(8,128)(2,1)} %concatenate.118, bf16[1024,1024]{0,1:T(8,128)(2,1)S(1)} %copy-done.17, f32[1024]{0:T(1024)S(1)} %copy-done.81, f32[1024]{0:T(1024)S(1)} %copy-done.83), kind=kOutput, calls=%fused_computation.318 | convolution fusion | flops 4838391808 | bytes 20979712 | tf_op jit(solution)/shard_map/dot_general | solution.py:421
  535.1 8.6 %convolution_convert_fusion.3 = bf16[1024,1024]{0,1:T(8,128)(2,1)} fusion(bf16[1024,2304]{1,0:T(8,128)(2,1)S(1)} %copy-done.54, bf16[1024,2304]{1,0:T(8,128)(2,1)} %all-gather.3.cloned.1.call-done), kind=kOutput, calls=%fused_computation.77 | convolution fusion | flops 4832886784 | bytes 11534336 | tf_op jit(solution)/shard_map/dot_general | solution.py:427
  568.1 25.2 %collective-permute-done.15 = bf16[2,64,768]{2,1,0:T(8,128)(2,1)S(1)} collective-permute-done((bf16[2,64,768]{2,1,0:T(8,128)(2,1)S(1)}, bf16[2,64,768]{2,1,0:T(8,128)(2,1)S(1)}, u32[]{:S(2)}, u32[]{:S(2)}) %collective-permute-start.15) | collective-permute-done | bytes 196640 | tf_op jit(solution)/shard_map/ppermute | solution.py:452
  599.1 5.7 collective-permute-done.12
  611.5 5.9 collective-permute-done.28
  617.9 9.2 %collective-permute-done.24 = bf16[2,64,1408]{2,1,0:T(8,128)(2,1)S(1)} collective-permute-done((bf16[2,64,1408]{2,1,0:T(8,128)(2,1)S(1)}, bf16[2,64,1408]{2,1,0:T(8,128)(2,1)S(1)}, u32[]{:S(2)}, u32[]{:S(2)}) %collective-permute-start.24) | collective-permute-done | bytes 360480 | tf_op jit(solution)/shard_map/ppermute | solution.py:452
  633.0 5.7 fusion.5
  638.7 5.4 copy.350
  650.4 17.0 %collective-permute-done.5 = bf16[2,2,2,64,768]{4,3,1,2,0:T(8,128)(2,1)S(1)} collective-permute-done((bf16[2,2,2,64,768]{4,3,1,2,0:T(8,128)(2,1)S(1)}, bf16[2,2,2,64,768]{4,3,1,2,0:T(8,128)(2,1)S(1)}, u32[]{:S(2)}, u32[]{:S(2)}) %collective-permute-start.5) | collective-permute-done | bytes 786464 | tf_op jit(solution)/shard_map/ppermute | solution.py:452
  669.8 17.0 %collective-permute-done.6 = bf16[2,2,64,768]{3,2,0,1:T(8,128)(2,1)S(1)} collective-permute-done((bf16[2,2,64,768]{3,2,0,1:T(8,128)(2,1)S(1)}, bf16[2,2,64,768]{3,2,0,1:T(8,128)(2,1)S(1)}, u32[]{:S(2)}, u32[]{:S(2)}) %collective-permute-start.6) | collective-permute-done | bytes 393248 | tf_op jit(solution)/shard_map/ppermute | solution.py:452
  (557 shorter events, 252.5 us)
Async XLA Ops:
  7.2 89.0 %all-gather.3.cloned.1.call-start = ((), (), s32[]{:S(2)}) async-start(), calls=%async_computation | async-start | bytes 5013504 | tf_op jit(solution)/shard_map/all_gather | solution.py:532
  13.0 198.1 %all-gather.5.cloned.1.call-start = ((), (), s32[]{:S(2)}) async-start(), calls=%async_computation.1 | async-start | bytes 8912896 | tf_op jit(solution)/shard_map/all_gather | solution.py:535
  247.3 31.1 %collective-permute-start.30 = (bf16[2,2,2,64,1280]{4,3,0,1,2:T(8,128)(2,1)}, bf16[2,2,2,64,1280]{4,3,0,1,2:T(8,128)(2,1)}, u32[]{:S(2)}, u32[]{:S(2)}) collective-permute-start(bf16[2,2,2,64,1280]{4,3,0,1,2:T(8,128)(2,1)} %bitcast.295), channel_id=1, source_target_pairs={{0,2},{2,0},{4,6},{6,4},{1,3},{3,1},{5,7},{7,5},{8,10},{10,8},{12,... | collective-permute-start | bytes 3932168 | tf_op jit(solution)/shard_map/ppermute | solution.py:452
  258.0 44.2 %collective-permute-start.2 = (bf16[1024,1024]{0,1:T(8,128)(2,1)}, bf16[1024,1024]{0,1:T(8,128)(2,1)}, u32[]{:S(2)}, u32[]{:S(2)}) collective-permute-start(bf16[1024,1024]{0,1:T(8,128)(2,1)} %fusion.28), channel_id=1, source_target_pairs={{0,1},{1,0},{2,3},{3,2},{4,5},{5,4},{6,7},{7,6},{8,9},{9,8},{10,11... | collective-permute-start | bytes 6291464 | tf_op jit(solution)/shard_map/ppermute | solution.py:437
  282.0 16.9 %collective-permute-start.31 = (bf16[2,2,64,1280]{3,2,0,1:T(8,128)(2,1)}, bf16[2,2,64,1280]{3,2,0,1:T(8,128)(2,1)}, u32[]{:S(2)}, u32[]{:S(2)}) collective-permute-start(bf16[2,2,64,1280]{3,2,0,1:T(8,128)(2,1)} %dynamic-slice_bitcast_fusion.4), channel_id=1, source_target_pairs={{0,4},{2,6},{4,0},{6,2},{1,5},{3,7},{5,1},{7,3},{8,12},{10,14},{12... | collective-permute-start | bytes 1966088 | tf_op jit(solution)/shard_map/ppermute | solution.py:452
  288.9 17.9 %collective-permute-start.1 = (bf16[1024,1024]{0,1:T(8,128)(2,1)}, bf16[1024,1024]{0,1:T(8,128)(2,1)}, u32[]{:S(2)}, u32[]{:S(2)}) collective-permute-start(bf16[1024,1024]{0,1:T(8,128)(2,1)} %convolution_convert_fusion.4), channel_id=1, source_target_pairs={{0,1},{1,0},{2,3},{3,2},{4,5},{5,4},{6,7},{7,6},{8,9},{9,8},{10,11... | collective-permute-start | bytes 6291464 | tf_op jit(solution)/shard_map/ppermute | solution.py:437
  301.8 202.8 %collective-permute-start.32 = (bf16[2,64,1280]{2,1,0:T(8,128)(2,1)}, bf16[2,64,1280]{2,1,0:T(8,128)(2,1)}, u32[]{:S(2)}, u32[]{:S(2)}) collective-permute-start(bf16[2,64,1280]{2,1,0:T(8,128)(2,1)} %dynamic-slice_bitcast_fusion.10), channel_id=1, source_target_pairs={{0,8},{8,0},{16,24},{24,16},{1,9},{9,1},{17,25},{25,17},{2,10},{10... | collective-permute-start | bytes 983048 | tf_op jit(solution)/shard_map/ppermute | solution.py:452
  402.3 112.0 %collective-permute-start.3 = (bf16[1024,256]{1,0:T(8,128)(2,1)}, bf16[1024,256]{1,0:T(8,128)(2,1)}, u32[]{:S(2)}, u32[]{:S(2)}) collective-permute-start(bf16[1024,256]{1,0:T(8,128)(2,1)} %get-tuple-element.213), channel_id=1, source_target_pairs={{0,1},{1,0},{2,3},{3,2},{4,5},{5,4},{6,7},{7,6},{8,9},{9,8},{10,11... | collective-permute-start | bytes 1572872 | tf_op jit(solution)/shard_map/ppermute | solution.py:437
  452.3 12.5 %collective-permute-start.17 = (f32[4,256]{1,0:T(4,128)S(1)}, f32[4,256]{1,0:T(4,128)S(1)}, u32[]{:S(2)}, u32[]{:S(2)}) collective-permute-start(f32[4,256]{1,0:T(4,128)S(1)} %pad_add_fusion.2), channel_id=1, source_target_pairs={{0,1},{1,0},{2,3},{3,2},{4,5},{5,4},{6,7},{7,6},{8,9},{9,8},{10,11... | collective-permute-start | bytes 12296 | tf_op jit(solution)/shard_map/ppermute | solution.py:652
  457.6 93.0 %collective-permute-start.26 = (bf16[2,2,2,64,1408]{4,3,1,2,0:T(8,128)(2,1)}, bf16[2,2,2,64,1408]{4,3,1,2,0:T(8,128)(2,1)}, u32[]{:S(2)}, u32[]{:S(2)}) collective-permute-start(bf16[2,2,2,64,1408]{4,3,1,2,0:T(8,128)(2,1)} %bitcast.293), channel_id=1, source_target_pairs={{0,8},{8,0},{16,24},{24,16},{1,9},{9,1},{17,25},{25,17},{2,10},{10... | collective-permute-start | bytes 4325384 | tf_op jit(solution)/shard_map/ppermute | solution.py:452
  461.9 93.6 %collective-permute-start.22 = (bf16[2,2,2,64,1408]{4,3,2,0,1:T(8,128)(2,1)}, bf16[2,2,2,64,1408]{4,3,2,0,1:T(8,128)(2,1)}, u32[]{:S(2)}, u32[]{:S(2)}) collective-permute-start(bf16[2,2,2,64,1408]{4,3,2,0,1:T(8,128)(2,1)} %bitcast.294), channel_id=1, source_target_pairs={{0,4},{2,6},{4,0},{6,2},{1,5},{3,7},{5,1},{7,3},{8,12},{10,14},{12... | collective-permute-start | bytes 4325384 | tf_op jit(solution)/shard_map/ppermute | solution.py:452
  468.8 27.2 %collective-permute-start.19 = (f32[4132]{0:T(1024)S(1)}, f32[4132]{0:T(1024)S(1)}, u32[]{:S(2)}, u32[]{:S(2)}) collective-permute-start(f32[4132]{0:T(1024)S(1)} %add.476), channel_id=1, source_target_pairs={{0,4},{2,6},{4,0},{6,2},{1,5},{3,7},{5,1},{7,3},{8,12},{10,14},{12... | collective-permute-start | bytes 49592 | tf_op jit(solution)/shard_map/ppermute | solution.py:452
  499.8 4.8 collective-permute-start.21
  505.7 7.8 %collective-permute-start.33 = (bf16[64,1280]{1,0:T(8,128)(2,1)S(1)}, bf16[64,1280]{1,0:T(8,128)(2,1)S(1)}, u32[]{:S(2)}, u32[]{:S(2)}) collective-permute-start(bf16[64,1280]{1,0:T(8,128)(2,1)S(1)} %dynamic-slice_bitcast_fusion.16), channel_id=1, source_target_pairs={{0,16},{8,24},{16,0},{24,8},{1,17},{9,25},{17,1},{25,9},{2,18},{10... | collective-permute-start | bytes 491528 | tf_op jit(solution)/shard_map/ppermute | solution.py:452
  532.8 15.4 %collective-permute-start.13 = (bf16[2,2,2,64,768]{4,3,2,1,0:T(8,128)(2,1)S(1)}, bf16[2,2,2,64,768]{4,3,2,1,0:T(8,128)(2,1)S(1)}, u32[]{:S(2)}, u32[]{:S(2)}) collective-permute-start(bf16[2,2,2,64,768]{4,3,2,1,0:T(8,128)(2,1)S(1)} %dynamic-slice_bitcast_fusion), channel_id=1, source_target_pairs={{0,4},{2,6},{4,0},{6,2},{1,5},{3,7},{5,1},{7,3},{8,12},{10,14},{12... | collective-permute-start | bytes 2359304 | tf_op jit(solution)/shard_map/ppermute | solution.py:452
  533.9 15.1 %collective-permute-start.9 = (bf16[2,2,2,64,768]{4,3,0,1,2:T(8,128)(2,1)S(1)}, bf16[2,2,2,64,768]{4,3,0,1,2:T(8,128)(2,1)S(1)}, u32[]{:S(2)}, u32[]{:S(2)}) collective-permute-start(bf16[2,2,2,64,768]{4,3,0,1,2:T(8,128)(2,1)S(1)} %bitcast.324), channel_id=1, source_target_pairs={{0,2},{2,0},{4,6},{6,4},{1,3},{3,1},{5,7},{7,5},{8,10},{10,8},{12,... | collective-permute-start | bytes 2359304 | tf_op jit(solution)/shard_map/ppermute | solution.py:452
  543.8 84.9 %collective-permute-start.4 = (bf16[1024,1024]{0,1:T(8,128)(2,1)}, bf16[1024,1024]{0,1:T(8,128)(2,1)}, u32[]{:S(2)}, u32[]{:S(2)}) collective-permute-start(bf16[1024,1024]{0,1:T(8,128)(2,1)} %convolution_convert_fusion.3), channel_id=1, source_target_pairs={{0,1},{1,0},{2,3},{3,2},{4,5},{5,4},{6,7},{7,6},{8,9},{9,8},{10,11... | collective-permute-start | bytes 6291464 | tf_op jit(solution)/shard_map/ppermute | solution.py:437
  548.5 15.8 %collective-permute-start.14 = (bf16[2,2,64,768]{3,2,1,0:T(8,128)(2,1)S(1)}, bf16[2,2,64,768]{3,2,1,0:T(8,128)(2,1)S(1)}, u32[]{:S(2)}, u32[]{:S(2)}) collective-permute-start(bf16[2,2,64,768]{3,2,1,0:T(8,128)(2,1)S(1)} %dynamic-slice_bitcast_fusion.5), channel_id=1, source_target_pairs={{0,8},{8,0},{16,24},{24,16},{1,9},{9,1},{17,25},{25,17},{2,10},{10... | collective-permute-start | bytes 1179656 | tf_op jit(solution)/shard_map/ppermute | solution.py:452
  549.2 16.2 %collective-permute-start.10 = (bf16[2,2,64,768]{3,2,0,1:T(8,128)(2,1)S(1)}, bf16[2,2,64,768]{3,2,0,1:T(8,128)(2,1)S(1)}, u32[]{:S(2)}, u32[]{:S(2)}) collective-permute-start(bf16[2,2,64,768]{3,2,0,1:T(8,128)(2,1)S(1)} %dynamic-slice_bitcast_fusion.6), channel_id=1, source_target_pairs={{0,4},{2,6},{4,0},{6,2},{1,5},{3,7},{5,1},{7,3},{8,12},{10,14},{12... | collective-permute-start | bytes 1179656 | tf_op jit(solution)/shard_map/ppermute | solution.py:452
  553.2 54.4 %collective-permute-start.27 = (bf16[2,2,64,1408]{3,2,0,1:T(8,128)(2,1)}, bf16[2,2,64,1408]{3,2,0,1:T(8,128)(2,1)}, u32[]{:S(2)}, u32[]{:S(2)}) collective-permute-start(bf16[2,2,64,1408]{3,2,0,1:T(8,128)(2,1)} %dynamic-slice_bitcast_fusion.2), channel_id=1, source_target_pairs={{0,16},{8,24},{16,0},{24,8},{1,17},{9,25},{17,1},{25,9},{2,18},{10... | collective-permute-start | bytes 2162696 | tf_op jit(solution)/shard_map/ppermute | solution.py:452
  558.2 51.9 %collective-permute-start.23 = (bf16[2,2,64,1408]{3,2,1,0:T(8,128)(2,1)}, bf16[2,2,64,1408]{3,2,1,0:T(8,128)(2,1)}, u32[]{:S(2)}, u32[]{:S(2)}) collective-permute-start(bf16[2,2,64,1408]{3,2,1,0:T(8,128)(2,1)} %dynamic-slice_bitcast_fusion.3), channel_id=1, source_target_pairs={{0,8},{8,0},{16,24},{24,16},{1,9},{9,1},{17,25},{25,17},{2,10},{10... | collective-permute-start | bytes 2162696 | tf_op jit(solution)/shard_map/ppermute | solution.py:452
  564.5 28.8 %collective-permute-start.15 = (bf16[2,64,768]{2,1,0:T(8,128)(2,1)S(1)}, bf16[2,64,768]{2,1,0:T(8,128)(2,1)S(1)}, u32[]{:S(2)}, u32[]{:S(2)}) collective-permute-start(bf16[2,64,768]{2,1,0:T(8,128)(2,1)S(1)} %dynamic-slice_bitcast_fusion.11), channel_id=1, source_target_pairs={{0,16},{8,24},{16,0},{24,8},{1,17},{9,25},{17,1},{25,9},{2,18},{10... | collective-permute-start | bytes 589832 | tf_op jit(solution)/shard_map/ppermute | solution.py:452
  565.5 32.7 %collective-permute-start.11 = (bf16[2,64,768]{2,1,0:T(8,128)(2,1)S(1)}, bf16[2,64,768]{2,1,0:T(8,128)(2,1)S(1)}, u32[]{:S(2)}, u32[]{:S(2)}) collective-permute-start(bf16[2,64,768]{2,1,0:T(8,128)(2,1)S(1)} %dynamic-slice_bitcast_fusion.12), channel_id=1, source_target_pairs={{0,8},{8,0},{16,24},{24,16},{1,9},{9,1},{17,25},{25,17},{2,10},{10... | collective-permute-start | bytes 589832 | tf_op jit(solution)/shard_map/ppermute | solution.py:452
  593.4 5.6 collective-permute-start.16
  598.3 6.4 collective-permute-start.12
  609.0 8.4 %collective-permute-start.28 = (bf16[2,64,1408]{2,1,0:T(8,128)(2,1)S(1)}, bf16[2,64,1408]{2,1,0:T(8,128)(2,1)S(1)}, u32[]{:S(2)}, u32[]{:S(2)}) collective-permute-start(bf16[2,64,1408]{2,1,0:T(8,128)(2,1)S(1)} %dynamic-slice_bitcast_fusion.8), channel_id=1, source_target_pairs={{0,2},{2,0},{4,6},{6,4},{1,3},{3,1},{5,7},{7,5},{8,10},{10,8},{12,... | collective-permute-start | bytes 1081352 | tf_op jit(solution)/shard_map/ppermute | solution.py:452
  611.4 15.6 %collective-permute-start.24 = (bf16[2,64,1408]{2,1,0:T(8,128)(2,1)S(1)}, bf16[2,64,1408]{2,1,0:T(8,128)(2,1)S(1)}, u32[]{:S(2)}, u32[]{:S(2)}) collective-permute-start(bf16[2,64,1408]{2,1,0:T(8,128)(2,1)S(1)} %dynamic-slice_bitcast_fusion.9), channel_id=1, source_target_pairs={{0,16},{8,24},{16,0},{24,8},{1,17},{9,25},{17,1},{25,9},{2,18},{10... | collective-permute-start | bytes 1081352 | tf_op jit(solution)/shard_map/ppermute | solution.py:452
  617.6 30.8 %collective-permute-start.29 = (bf16[64,1408]{1,0:T(8,128)(2,1)S(1)}, bf16[64,1408]{1,0:T(8,128)(2,1)}, u32[]{:S(2)}, u32[]{:S(2)}) collective-permute-start(bf16[64,1408]{1,0:T(8,128)(2,1)S(1)} %dynamic-slice_bitcast_fusion.14), channel_id=1, source_target_pairs={{0,4},{2,6},{4,0},{6,2},{1,5},{3,7},{5,1},{7,3},{8,12},{10,14},{12... | collective-permute-start | bytes 540680 | tf_op jit(solution)/shard_map/ppermute | solution.py:452
  627.9 21.5 %collective-permute-start.25 = (bf16[64,1408]{1,0:T(8,128)(2,1)}, bf16[64,1408]{1,0:T(8,128)(2,1)}, u32[]{:S(2)}, u32[]{:S(2)}) collective-permute-start(bf16[64,1408]{1,0:T(8,128)(2,1)} %dynamic-slice_bitcast_fusion.15), channel_id=1, source_target_pairs={{0,2},{2,0},{4,6},{6,4},{1,3},{3,1},{5,7},{7,5},{8,10},{10,8},{12,... | collective-permute-start | bytes 540680 | tf_op jit(solution)/shard_map/ppermute | solution.py:452
  648.3 19.1 %collective-permute-start.5 = (bf16[2,2,2,64,768]{4,3,1,2,0:T(8,128)(2,1)S(1)}, bf16[2,2,2,64,768]{4,3,1,2,0:T(8,128)(2,1)S(1)}, u32[]{:S(2)}, u32[]{:S(2)}) collective-permute-start(bf16[2,2,2,64,768]{4,3,1,2,0:T(8,128)(2,1)S(1)} %dynamic-slice_bitcast_fusion.1), channel_id=1, source_target_pairs={{0,8},{8,0},{16,24},{24,16},{1,9},{9,1},{17,25},{25,17},{2,10},{10... | collective-permute-start | bytes 2359304 | tf_op jit(solution)/shard_map/ppermute | solution.py:452
  667.7 19.1 %collective-permute-start.6 = (bf16[2,2,64,768]{3,2,0,1:T(8,128)(2,1)S(1)}, bf16[2,2,64,768]{3,2,0,1:T(8,128)(2,1)S(1)}, u32[]{:S(2)}, u32[]{:S(2)}) collective-permute-start(bf16[2,2,64,768]{3,2,0,1:T(8,128)(2,1)S(1)} %dynamic-slice_bitcast_fusion.7), channel_id=1, source_target_pairs={{0,16},{8,24},{16,0},{24,8},{1,17},{9,25},{17,1},{25,9},{2,18},{10... | collective-permute-start | bytes 1179656 | tf_op jit(solution)/shard_map/ppermute | solution.py:452
  686.9 6.8 collective-permute-start.7
  (128 other events, 1653.1 us)
Sparse Core Ops, SparseCore 0:
  13.1 83.0 all-gather.2
  99.5 111.4 all-gather.4
